TPU v7x, 512 devices: a whole 4x8x8 slice. The times are simulated.
512 devices in a mesh: frames: 64 (over z, y_hi, core), coords: 8 (over y_lo, x).
Axes of the slice: x: 4, y: 8 (y_hi: 4, y_lo: 2; y = y_hi * 2 + y_lo), z: 8, core: 2. Of those that a mesh axis runs over, the one named last changes fastest.
Arguments:
- frames_xyz: bfloat16 [6144, 3, 65536], P('frames', None, 'coords'), may hold values from -120 to 120
- mean_xyz: float32 [3, 65536], P(None, 'coords'), may hold values from -60 to 60
- vector_block: bfloat16 [32, 3, 65536], P(None, None, ('coords', 'frames')), may hold values from -6 to 6
Outputs:
- product: float32 [32, 3, 65536], P(None, None, ('coords', 'frames'))
All inputs are finite; a program needn't handle non-finite values.
Results may differ from a plain program's by a relative error of at most 0.0049.
Values may be sent and summed in bfloat16 or wider, within the bound.
No kernel may reach another device: no remote copies, remote signals or barrier semaphores. Data moves between devices by JAX's collectives and lax.ppermute only.
A program may use at most 64 MiB of HBM per device.

v0:
```python
import jax
import jax.numpy as jnp
from jax import lax
from jax.sharding import PartitionSpec as P

NATOM = 65536
NS_STEPS = 8


def polar_factor(amat):
    for step in range(NS_STEPS):
        square = jnp.einsum("ijf,kjf->ikf", amat, amat, precision=lax.Precision.HIGHEST)
        amat = 1.5 * amat - 0.5 * jnp.einsum(
            "ikf,kjf->ijf", square, amat, precision=lax.Precision.HIGHEST
        )
    return amat


def body(frames_xyz, mean_xyz, vector_block):
    coords = frames_xyz.astype(jnp.float32)
    local_sums = jnp.sum(coords, axis=2)
    local_cross = jnp.einsum("fja,ia->ijf", coords, mean_xyz, precision=lax.Precision.HIGHEST)
    mean_sums = jnp.sum(mean_xyz, axis=1)
    total_sums, total_cross, total_mean = lax.psum((local_sums, local_cross, mean_sums), "coords")
    centre = total_mean / NATOM
    cross = total_cross - centre[:, None, None] * total_sums.T[None, :, :]
    scale_frob = jnp.sqrt(1.0 + jnp.sum(cross * cross, axis=(0, 1)))
    rotation = polar_factor(cross / scale_frob[None, None, :])
    shifted = coords - (total_sums / NATOM)[:, :, None]
    deviation = jnp.einsum("ijf,fja->fia", rotation, shifted, precision=lax.Precision.HIGHEST)
    deviation = (deviation - (mean_xyz - centre[:, None])[None]).astype(jnp.bfloat16)
    partial_proj = jnp.einsum(
        "fia,kia->fk",
        deviation,
        lax.all_gather(vector_block, "frames", axis=2, tiled=True),
        preferred_element_type=jnp.float32,
    )
    projection = lax.psum(partial_proj, "coords").astype(jnp.bfloat16)
    term = jnp.einsum("fk,fia->kia", projection, deviation, preferred_element_type=jnp.float32)
    frame_count = deviation.shape[0] * lax.axis_size("frames")
    width_own = vector_block.shape[2]
    summed = lax.psum(term, "frames")
    offset = lax.axis_index("frames") * width_own
    mine = lax.dynamic_slice_in_dim(summed, offset, width_own, 2)
    return mine / frame_count


def solution(mesh):
    in_specs = (P("frames", None, "coords"), P(None, "coords"), P(None, None, ("coords", "frames")))
    out_specs = P(None, None, ("coords", "frames"))
    return jax.shard_map(body, mesh=mesh, in_specs=in_specs, out_specs=out_specs, check_vma=False)
```

profile of v0, /device:TPU:1, one launch (start us, length us, event | category | flops | bytes accessed | tf_op | source)
XLA Modules:
  0.0 717.6 jit_solution(1148278988550171243)
XLA Ops:
  7.3 3.1 convert_reduce_fusion
  10.4 6.6 convolution_bitcast_fusion.8
  17.1 17.4 %all-reduce = (f32[3,3,96]{2,0,1:T(4,128)S(1)}, f32[96,3]{0,1:T(4,128)S(1)}, f32[3]{0:T(128)S(1)}) all-reduce(f32[3,3,96]{2,0,1:T(4,128)S(1)} %convolution_bitcast_fusion.8, f32[96,3]{0,1:T(4,128)S(1)} %convert_reduce_fusion, f32[3]{0:T(128)S(1)} %reduce_sum.27), channel_id=1, replica_groups=mesh['frames'=64,'coords'=8] {'coords'}, use_global_device_ids=true, to_apply=%region_0.0 | all-reduce | flops 1155 | bytes 9240 | tf_op jit(solution)/shard_map/psum | solution.py:24
  34.9 0.9 convolution_bitcast_fusion.7
  35.9 0.8 fusion.15
  37.0 0.9 convolution_bitcast_fusion.6
  39.0 0.9 convolution_bitcast_fusion.5
  39.9 0.8 fusion.17
  41.0 0.9 convolution_bitcast_fusion.4
  41.9 0.8 fusion.18
  43.0 0.9 convolution_bitcast_fusion.3
  45.0 0.9 convolution_bitcast_fusion.2
  45.9 0.8 fusion.20
  47.0 1.1 convolution_bitcast_fusion.1
  48.1 0.8 fusion.21
  49.2 0.9 convolution_bitcast_fusion
  51.2 3.6 convert_subtract_fusion
  54.8 30.4 %subtract_convert_fusion = bf16[96,3,8192]{2,1,0:T(4,128)(2,1)} fusion(f32[3,3,96]{1,0,2:T(4,128)S(1)} %copy.18, f32[96,3,8192]{2,0,1:T(8,128)S(1)} %convert_subtract_fusion, f32[3,8192]{1,0:T(4,128)S(1)} %broadcast_subtract_fusion), kind=kOutput, calls=%fused_computation.2 | convolution fusion | flops 89653248 | bytes 14257536 | tf_op jit(solution)/shard_map/ijf,fja->fia/dot_general | solution.py:30
  85.3 10.0 %all-gather.2.cloned.1.call-done = bf16[32,3,8192]{2,0,1:T(8,128)(2,1)} async-done(((bf16[32,3,128]{2,0,1:T(8,128)(2,1)}), bf16[32,3,8192]{2,0,1:T(8,128)(2,1)}) %all-gather.2.cloned.1.call-update) | async-done | bytes 1572880 | tf_op jit(solution)/shard_map/all_gather | solution.py:35
  95.3 8.4 %fusion.8 = f32[96,32]{0,1:T(8,128)S(1)} fusion(bf16[32,3,8192]{2,0,1:T(8,128)(2,1)} %all-gather.2.cloned.1.call-done, bf16[96,3,8192]{2,1,0:T(4,128)(2,1)} %subtract_convert_fusion), kind=kOutput, calls=%fused_computation.17 | convolution fusion | flops 150994944 | bytes 6303744 | tf_op jit(solution)/shard_map/fia,kia->fk/dot_general | solution.py:32
  103.7 26.2 %psum.38 = bf16[96,32]{0,1:T(8,128)(2,1)S(1)} all-reduce(f32[96,32]{0,1:T(8,128)S(1)} %fusion.8), channel_id=1, replica_groups=mesh['frames'=64,'coords'=8] {'coords'}, use_global_device_ids=true, to_apply=%region_6.0 | all-reduce | flops 3072 | bytes 18432 | tf_op jit(solution)/shard_map/psum | solution.py:38
  129.9 10.0 %fusion.6 = f32[32,3,8192]{2,0,1:T(8,128)} fusion(bf16[96,3,8192]{2,1,0:T(4,128)(2,1)} %subtract_convert_fusion, bf16[96,32]{0,1:T(8,128)(2,1)S(1)} %psum.38), kind=kOutput, calls=%fused_computation.7 | convolution fusion | flops 150994944 | bytes 7870464 | tf_op jit(solution)/shard_map/fk,fia->kia/dot_general | solution.py:39
  139.9 569.0 %all-reduce.3.cloned.1.call-done = f32[32,3,8192]{2,0,1:T(8,128)} async-done(((f32[32,3,8192]{2,0,1:T(8,128)}), f32[32,3,8192]{2,0,1:T(8,128)}) %all-reduce.3.cloned.1.call-update) | async-done | bytes 3145744 | tf_op jit(solution)/shard_map/psum | solution.py:42
  708.9 1.4 dynamic-slice_multiply_fusion
  (41 shorter events, 5.9 us)
Async XLA Ops:
  6.5 10.4 %copy-start = (f32[3,8192]{1,0:T(4,128)S(1)}, f32[3,8192]{1,0:T(4,128)}, u32[]{:S(2)}) copy-start(f32[3,8192]{1,0:T(4,128)} %param.4) | copy-start | bytes 294916
  6.5 88.8 %all-gather.2.cloned.1.call-start = ((), (), s32[]{:S(2)}) async-start(), calls=%async_computation | async-start | bytes 1597440 | tf_op jit(solution)/shard_map/all_gather | solution.py:35
  7.3 701.7 %all-reduce.3.cloned.1.call-start = ((), (), s32[]{:S(2)}) async-start(), calls=%async_computation.1 | async-start | bytes 6291456 | tf_op jit(solution)/shard_map/psum | solution.py:42
Sparse Core Ops, SparseCore 0:
  10.6 84.6 all-gather.1
  140.0 568.8 all-reduce.2
where the time goes:
time: 721 us; the launch traced here: 718 us
  waiting for transfers between devices  580 us (80%)
  matrix products  69.3 us (10%)
  blocking collectives  43.6 us (6%)
  between operations  14.1 us (2%)
  other arithmetic  8.64 us (1%)
    psum x1, waiting for transfers between devices, body(): summed = lax.psum(term, 'frames')  569 us
    dot_general x1, matrix products, body(): jnp.einsum('ijf,fja->fia', rotation, shifted, precision=lax.Precision.HIG...  30.4 us
    psum x1, blocking collectives, body(): projection = lax.psum(partial_proj, 'coords').astype(jnp.bfloat16)  26.2 us
    psum x1, blocking collectives, body(): lax.psum((local_sums, local_cross, mean_sums), 'coords')  17.4 us
  transfers between devices with their start and end apart: 2, of which 2 were waited for; matrix products, arithmetic and copies ran while one was open for 8% of the time, Pallas kernels for 0%

commit v1 on v0

v1 whole, which is shorter than its diff:
```python
import functools

import jax
import jax.numpy as jnp
from jax import lax
from jax.experimental import pallas as pl
from jax.experimental.pallas import tpu as pltpu
from jax.sharding import Mesh
from jax.sharding import PartitionSpec as P

NS_STEPS = 8
LANES = 128
PAIR = 256
EXTRA = 16
F32 = jnp.float32
BF16 = jnp.bfloat16
HIGHEST = lax.Precision.HIGHEST
NT = (((1,), (1,)), ((), ()))
TN = (((0,), (0,)), ((), ()))


def iota(shape, dim):
    return lax.broadcasted_iota(jnp.int32, shape, dim)


def split3(value):
    high = value.astype(BF16)
    rest = value - high.astype(F32)
    middle = rest.astype(BF16)
    low = (rest - middle.astype(F32)).astype(BF16)
    return high, middle, low


def mean_rows(mean16):
    high, middle, low = split3(mean16)
    row = iota(mean16.shape, 0)
    take = jnp.where(row < 3, high.astype(F32), jnp.where(row < 6, middle.astype(F32), jnp.where(row < 9, low.astype(F32), mean16)))
    return take.astype(BF16)


def cross_kernel(core_ref, x_ref, mean_ref, keep_ref, send_ref, rows_ref, cross_ref, acc_ref):
    step = pl.program_id(0)
    core = core_ref[0]
    extra = mean_rows(mean_ref[...])
    width = x_ref.shape[1]

    @pl.when(step == 0)
    def _():
        acc_ref[...] = jnp.zeros_like(acc_ref)

    total = acc_ref[...]
    for pair in range(width // PAIR):
        columns = slice(pair * PAIR, (pair + 1) * PAIR)
        side = extra[:, columns]
        left = jnp.concatenate([x_ref[:, columns], side], axis=0)
        total += lax.dot_general(left, side, NT, preferred_element_type=F32)
        block = slice(pair * LANES, (pair + 1) * LANES)
        first, second = left[:-EXTRA, :LANES], left[:-EXTRA, LANES:]
        keep_ref[:, block] = jnp.where(core == 0, first, second)
        send_ref[:, block] = jnp.where(core == 0, second, first)
        rows_ref[:, block] = jnp.where(core == 0, side[:, :LANES], side[:, LANES:])
    acc_ref[...] = total

    @pl.when(step == pl.num_programs(0) - 1)
    def _():
        row, col = iota((8, EXTRA), 0), iota((8, EXTRA), 1)
        pick = ((row < 3) & (col < 9) & ((col == row) | (col == row + 3) | (col == row + 6))) | ((row == 3) & (col == 9))
        cross_ref[...] = lax.dot_general(pick.astype(F32), total, NT, precision=HIGHEST, preferred_element_type=F32)


def polar_factor(amat):
    for _ in range(NS_STEPS):
        square = [[sum(amat[i][j] * amat[k][j] for j in range(3)) for k in range(3)] for i in range(3)]
        amat = [[1.5 * amat[i][j] - 0.5 * sum(square[i][k] * amat[k][j] for k in range(3)) for j in range(3)] for i in range(3)]
    return amat


def rotation_kernel(natom, core_ref, parts_ref, out_ref):
    core = core_ref[0]
    half = parts_ref.shape[0] // 2
    frames = (parts_ref.shape[2] - EXTRA) // 3
    lanes = out_ref.shape[1]
    first, second = parts_ref[0], parts_ref[half]
    for index in range(1, half):
        first += parts_ref[index]
        second += parts_ref[half + index]
    own = jnp.where(core == 0, first, second)
    other = jnp.where(core == 0, second, first)
    row, lane = iota((EXTRA, lanes), 0), iota((EXTRA, lanes), 1)
    third = lanes // 3
    which = (lane >= third).astype(jnp.int32) + (lane >= 2 * third).astype(jnp.int32)
    ones_at = 3 * frames + 9
    centre = [own[i : i + 1, ones_at : ones_at + 1] / natom for i in range(3)]
    for side, total in enumerate((own, other)):
        sums = [total[3:4, j * frames : (j + 1) * frames] for j in range(3)]
        cross = [[total[i : i + 1, j * frames : (j + 1) * frames] - centre[i] * sums[j] for j in range(3)] for i in range(3)]
        scale = jnp.sqrt(1.0 + sum(cross[i][j] * cross[i][j] for i in range(3) for j in range(3)))
        rotation = polar_factor([[cross[i][j] / scale for j in range(3)] for i in range(3)])
        shift = [sum(rotation[i][j] * (sums[j] / natom) for j in range(3)) for i in range(3)]
        entries = [rotation[i][j] for i in range(3) for j in range(3)] + shift
        at = iota((EXTRA, frames), 0)
        packed = jnp.zeros((EXTRA, frames), F32)
        for index, entry in enumerate(entries):
            packed = jnp.where(at == index, entry, packed)
        for index in range(4):
            chosen = (row == 3 * which + index) if index < 3 else (row == 9 + which)
            spread = lax.dot_general(packed, chosen.astype(F32), TN, precision=HIGHEST, preferred_element_type=F32)
            begin = (2 * index + side) * frames
            out_ref[begin : begin + frames, :] = spread
    which8 = which[:8]
    out_ref[8 * frames : 8 * frames + 8, :] = jnp.where(which8 == 0, centre[0], jnp.where(which8 == 1, centre[1], centre[2]))


def lane_part(shape):
    lane = iota(shape, 1)
    third = shape[1] // 3
    return (lane >= third).astype(jnp.int32) + (lane >= 2 * third).astype(jnp.int32)


def projection_kernel(core_ref, keep_ref, recv_ref, rows_ref, vec_ref, rot_ref, out_ref, acc_ref):
    step = pl.program_id(0)
    core = core_ref[0]

    @pl.when(step == 0)
    def _():
        acc_ref[...] = jnp.zeros_like(acc_ref)

    total = acc_ref[...]
    for pair in range(keep_ref.shape[1] // PAIR):
        columns = slice(pair * PAIR, (pair + 1) * PAIR)
        left = jnp.concatenate([keep_ref[:, columns], recv_ref[:, columns], rows_ref[:, columns]], axis=0)
        right = jnp.concatenate([vec_ref[2 * pair], vec_ref[2 * pair + 1]], axis=1)
        total += lax.dot_general(left, right, NT, preferred_element_type=F32)
    acc_ref[...] = total

    @pl.when(step == pl.num_programs(0) - 1)
    def _():
        frames = keep_ref.shape[0] // 3
        lanes = vec_ref.shape[1]
        third = lanes // 3
        extra = total[6 * frames :, :]
        vec_sums = extra[9:10, :]
        centre = rot_ref[8 * frames : 8 * frames + 1, :]
        part = lane_part((1, lanes))
        along = [extra[i : i + 1] + extra[3 + i : 4 + i] + extra[6 + i : 7 + i] for i in range(3)]
        mean_term = jnp.where(part == 0, along[0], jnp.where(part == 1, along[1], along[2])) - centre * vec_sums
        halves = []
        for side in range(2):
            value = -rot_ref[(6 + side) * frames : (7 + side) * frames, :] * vec_sums - mean_term
            for j in range(3):
                spread = rot_ref[(2 * j + side) * frames : (2 * j + side + 1) * frames, :]
                begin = (3 * side + j) * frames
                value += spread * total[begin : begin + frames, :]
            halves.append(value)
        first = jnp.where(core == 0, halves[0], halves[1])
        second = jnp.where(core == 0, halves[1], halves[0])
        value = jnp.concatenate([first, second], axis=0)
        quarter = frames // 2
        row, col = iota((lanes, 4 * third), 0), iota((lanes, 4 * third), 1)
        packed = jnp.zeros((quarter, 4 * third), F32)
        for q in range(4):
            fold = (row % third == col % third) & (col // third == q)
            packed += lax.dot_general(
                value[q * quarter : (q + 1) * quarter, :], fold.astype(F32), (((1,), (0,)), ((), ())),
                precision=HIGHEST, preferred_element_type=F32,
            )
        out_ref[...] = packed


def product_kernel(core_ref, parts_ref, rot_ref, keep_ref, recv_ref, rows_ref, out_ref, weight_ref):
    step = pl.program_id(0)
    frames = keep_ref.shape[0] // 3
    lanes = rot_ref.shape[1]
    third = lanes // 3

    @pl.when(step == 0)
    def _():
        core = core_ref[0]
        packed = parts_ref[0]
        for index in range(1, parts_ref.shape[0]):
            packed += parts_ref[index]
        packed = packed.astype(BF16)
        row, col = iota((4 * third, lanes), 0), iota((4 * third, lanes), 1)
        quarters = []
        for q in range(4):
            unfold = (row % third == col % third) & (row // third == q)
            quarters.append(jnp.dot(packed, unfold.astype(F32).astype(BF16), preferred_element_type=F32))
        first = jnp.concatenate(quarters[:2], axis=0)
        second = jnp.concatenate(quarters[2:], axis=0)
        sides = (jnp.where(core == 0, first, second), jnp.where(core == 0, second, first))
        centre = rot_ref[8 * frames : 8 * frames + 1, :]
        pieces = []
        proj_sum = jnp.zeros((1, lanes), F32)
        shift_sum = jnp.zeros((1, lanes), F32)
        for side in range(2):
            for j in range(3):
                begin = (2 * j + side) * frames
                pieces.append(rot_ref[begin : begin + frames, :] * sides[side])
            proj_sum += jnp.sum(sides[side], axis=0, keepdims=True)
            shift = rot_ref[(6 + side) * frames : (7 + side) * frames, :]
            shift_sum += jnp.sum(sides[side] * shift, axis=0, keepdims=True)
        at, part = iota((EXTRA, lanes), 0), lane_part((EXTRA, lanes))
        is_mean = (at < 9) & ((at == part) | (at == part + 3) | (at == part + 6))
        tail = jnp.where(is_mean, -proj_sum, jnp.where(at == 9, centre * proj_sum - shift_sum, 0.0))
        weight = jnp.concatenate(pieces + [tail], axis=0)
        same = (iota((lanes, lanes), 0) == iota((lanes, lanes), 1)).astype(F32).astype(BF16)
        for index, piece in enumerate(split3(weight)):
            turned = lax.dot_general(same, piece, NT, preferred_element_type=F32)
            weight_ref[index * lanes : (index + 1) * lanes, :] = turned.astype(BF16)

    weight = weight_ref[...]
    for pair in range(keep_ref.shape[1] // PAIR):
        columns = slice(pair * PAIR, (pair + 1) * PAIR)
        right = jnp.concatenate([keep_ref[:, columns], recv_ref[:, columns], rows_ref[:, columns]], axis=0)
        term = jnp.dot(weight, right, preferred_element_type=F32)
        term = (term[2 * lanes :] + term[lanes : 2 * lanes] + term[:lanes]).astype(BF16)
        out_ref[2 * pair] = term[:, :LANES]
        out_ref[2 * pair + 1] = term[:, LANES:]


VMEM_LIMIT = 40 * 1024 * 1024
SMEM_SPEC = pl.BlockSpec(memory_space=pltpu.SMEM)


def params():
    return pltpu.CompilerParams(vmem_limit_bytes=VMEM_LIMIT, dimension_semantics=("arbitrary",))


def cost(flops, moved):
    return pl.CostEstimate(flops=flops, bytes_accessed=moved, transcendentals=0)


def whole(*shape):
    return pl.BlockSpec(shape, lambda step: (0,) * len(shape))


def body(frames_xyz, mean_xyz, vector_block):
    frames, _, atoms = frames_xyz.shape
    kcount, _, own_atoms = vector_block.shape
    lanes = 3 * kcount
    rows = 3 * frames
    half = atoms // 2
    chips = half // own_atoms
    coords_size = lax.axis_size("yl") * lax.axis_size("x")
    peers = 2 * coords_size
    natom = atoms * coords_size
    frame_count = frames * 2 * chips
    core = lax.axis_index("core").astype(jnp.int32).reshape(1)
    x_rows = frames_xyz.transpose(1, 0, 2).reshape(rows, atoms)
    vec_rows = vector_block.transpose(1, 0, 2).reshape(lanes, own_atoms)
    vecs = lax.all_to_all(
        jnp.broadcast_to(vec_rows[None], (chips, lanes, own_atoms)), ("z", "yh"), 0, 0, tiled=True
    )
    mean16 = jnp.concatenate([mean_xyz] * 3 + [jnp.ones((1, atoms), F32), jnp.zeros((EXTRA - 10, atoms), F32)], axis=0)

    steps = max(1, atoms // 2048)
    wide, narrow = atoms // steps, half // steps
    columns = lambda height, width: pl.BlockSpec((height, width), lambda step: (0, step))
    keep, send, side, cross = pl.pallas_call(
        cross_kernel,
        grid=(steps,),
        in_specs=[SMEM_SPEC, columns(rows, wide), columns(EXTRA, wide)],
        out_specs=[columns(rows, narrow), columns(rows, narrow), columns(EXTRA, narrow), whole(8, rows + EXTRA)],
        out_shape=[
            jax.ShapeDtypeStruct((rows, half), BF16),
            jax.ShapeDtypeStruct((rows, half), BF16),
            jax.ShapeDtypeStruct((EXTRA, half), BF16),
            jax.ShapeDtypeStruct((8, rows + EXTRA), F32),
        ],
        scratch_shapes=[pltpu.VMEM((rows + EXTRA, EXTRA), F32)],
        compiler_params=params(),
        cost_estimate=cost(2 * rows * atoms * 256, 4 * rows * atoms),
        name="cross_terms",
    )(core, x_rows, mean16)
    recv = lax.ppermute(send, "core", [(0, 1), (1, 0)])
    parts = lax.all_to_all(
        jnp.broadcast_to(cross[None], (peers,) + cross.shape), ("core", "yl", "x"), 0, 0, tiled=True
    )
    rot = pl.pallas_call(
        functools.partial(rotation_kernel, natom),
        grid=(1,),
        in_specs=[SMEM_SPEC, whole(*parts.shape)],
        out_specs=whole(8 * frames + 8, lanes),
        out_shape=jax.ShapeDtypeStruct((8 * frames + 8, lanes), F32),
        compiler_params=params(),
        cost_estimate=cost(10**9, 10**6),
        name="rotation",
    )(core, parts)

    blocks = chips // steps
    vec_spec = pl.BlockSpec((blocks, lanes, LANES), lambda step: (step, 0, 0))
    proj = pl.pallas_call(
        projection_kernel,
        grid=(steps,),
        in_specs=[SMEM_SPEC, columns(rows, narrow), columns(rows, narrow), columns(EXTRA, narrow), vec_spec, whole(*rot.shape)],
        out_specs=whole(frames // 2, 4 * kcount),
        out_shape=jax.ShapeDtypeStruct((frames // 2, 4 * kcount), F32),
        scratch_shapes=[pltpu.VMEM((2 * rows + EXTRA, lanes), F32)],
        compiler_params=params(),
        cost_estimate=cost(4 * rows * half * 256, 4 * rows * half),
        name="projection",
    )(core, keep, recv, side, vecs, rot)
    proj_parts = lax.all_to_all(
        jnp.broadcast_to(proj[None], (peers,) + proj.shape), ("core", "yl", "x"), 0, 0, tiled=True
    )
    term = pl.pallas_call(
        product_kernel,
        grid=(steps,),
        in_specs=[
            SMEM_SPEC, whole(*proj_parts.shape), whole(*rot.shape),
            columns(rows, narrow), columns(rows, narrow), columns(EXTRA, narrow),
        ],
        out_specs=vec_spec,
        out_shape=jax.ShapeDtypeStruct((chips, lanes, LANES), BF16),
        scratch_shapes=[pltpu.VMEM((3 * lanes, 2 * rows + EXTRA), BF16)],
        compiler_params=params(),
        cost_estimate=cost(4 * rows * half * 288, 4 * rows * half),
        name="product_terms",
    )(core, proj_parts, rot, keep, recv, side)
    terms = lax.all_to_all(term, ("z", "yh"), 0, 0, tiled=True)
    total = jnp.sum(terms.astype(F32), axis=0) / frame_count
    return total.reshape(3, kcount, own_atoms).transpose(1, 0, 2)


def solution(mesh):
    sizes = mesh_sizes(mesh)
    inner = Mesh(mesh.devices.reshape(sizes), ("z", "yh", "core", "yl", "x"))
    frames, coords = ("z", "yh", "core"), ("yl", "x")
    in_specs = (P(frames, None, coords), P(None, coords), P(None, None, coords + frames))
    out_specs = P(None, None, coords + frames)
    return jax.shard_map(body, mesh=inner, in_specs=in_specs, out_specs=out_specs, check_vma=False)


def mesh_sizes(mesh):
    frames, coords = mesh.shape["frames"], mesh.shape["coords"]
    return (frames // 8, 4, 2, 2, coords // 2)
```

time: 721 us -> 123 us (0.17)
  waiting for transfers between devices: 580 us -> 21.7 us
  matrix products: 69.3 us -> 0 us
  starting transfers between devices: 0.04 us -> 20.4 us
  Pallas kernels: 0 us -> 16.1 us
  between operations: 14.1 us -> 0.09 us
  blocking collectives: 43.6 us -> 54.7 us
  other arithmetic: 8.64 us -> 0.74 us
    psum x1 -> x0, waiting for transfers between devices: 569 us -> none  [body(): summed = lax.psum(term, 'frames')]
    dot_general x20 -> x0, matrix products: 69.3 us -> none  [the longest x1 30.4 us: body(): jnp.einsum('ijf,fja->fia', rotation, shifted, precision=lax.Precision.HIG...]
    all_to_all x0 -> x3, blocking collectives: none -> 54.7 us  [the longest x1 31.1 us: body(): terms = lax.all_to_all(term, ('z', 'yh'), 0, 0, tiled=True)]
    psum x2 -> x0, blocking collectives: 43.6 us -> none  [the longest x1 26.2 us: body(): projection = lax.psum(partial_proj, 'coords').astype(jnp.bfloat16)]
    all_to_all x0 -> x1, waiting for transfers between devices: none -> 21.7 us  [body(): lax.all_to_all(jnp.broadcast_to(vec_rows[None], (chips, lanes, own_atoms)...]
    pallas_call x0 -> x4, Pallas kernels: none -> 16.1 us  [the longest x1 4.71 us: body(): pl.pallas_call(product_kernel, grid=(steps,), in_specs=[SMEM_SPEC, whole(...]
    all_to_all x0 -> x1, starting transfers between devices: none -> 11.6 us  [body(): lax.all_to_all(jnp.broadcast_to(vec_rows[None], (chips, lanes, own_atoms)...]
    all_gather x1 -> x0, waiting for transfers between devices: 10 us -> none  [body(): lax.all_gather(vector_block, 'frames', axis=2, tiled=True)]
  transfers between devices with their start and end apart: 2 -> 2, of which waited for: 2 -> 1; matrix products, arithmetic and copies ran while one was open for 8% -> 1% of each run, Pallas kernels for 0% -> 3%
where the time goes in v1:
time: 123 us
  blocking collectives  54.7 us (44%)
  waiting for transfers between devices  21.7 us (18%)
  starting transfers between devices  20.4 us (17%)
  Pallas kernels  16.1 us (13%)
  local copies, waits for them, and re-layouts  9.07 us (7%)
    all_to_all x1, blocking collectives, body(): terms = lax.all_to_all(term, ('z', 'yh'), 0, 0, tiled=True)  31.1 us
    all_to_all x1, waiting for transfers between devices, body(): lax.all_to_all(jnp.broadcast_to(vec_rows[None], (chips, lanes, own_atoms)...  21.7 us
    all_to_all x1, blocking collectives, body(): lax.all_to_all(jnp.broadcast_to(proj[None], (peers,) + proj.shape), ('cor...  13.4 us
    all_to_all x1, starting transfers between devices, body(): lax.all_to_all(jnp.broadcast_to(vec_rows[None], (chips, lanes, own_atoms)...  11.6 us
    all_to_all x1, blocking collectives, body(): lax.all_to_all(jnp.broadcast_to(cross[None], (peers,) + cross.shape), ('c...  10.2 us
    ppermute x1, starting transfers between devices, body(): recv = lax.ppermute(send, 'core', [(0, 1), (1, 0)])  8.79 us
    unnamed x10, local copies, waits for them, and re-layouts  4.83 us
    pallas_call x1, Pallas kernels, body(): pl.pallas_call(product_kernel, grid=(steps,), in_specs=[SMEM_SPEC, whole(...  4.71 us
  transfers between devices with their start and end apart: 2, of which 1 were waited for; matrix products, arithmetic and copies ran while one was open for 1% of the time, Pallas kernels for 3%

profile of v1, /device:TPU:1, one launch (start us, length us, event | category | flops | bytes accessed | tf_op | source)
XLA Modules:
  0.0 122.9 jit_solution(549171159421177766)
XLA Ops:
  0.0 3.1 %concatenate.3.mean_ref = f32[16,8192]{1,0:T(8,128)S(1)} concatenate(f32[3,8192]{1,0:T(4,128)} %param.4, f32[3,8192]{1,0:T(4,128)} %param.4, f32[3,8192]{1,0:T(4,128)} %param.4, f32[1,8192]{1,0:T(1,128)S(1)} %broadcast_in_dim.12, f32[6,8192]{1,0:T(8,128)S(1)} %broadcast_in_dim.26), dimensions={0} | concatenate | bytes 1048576 | tf_op jit(solution)/shard_map/concatenate | solution.py:254
  3.2 0.0 copy-start
  3.2 2.3 %copy-done = bf16[96,3,8192]{2,0,1:T(8,128)(2,1)S(1)} copy-done((bf16[96,3,8192]{2,0,1:T(8,128)(2,1)S(1)}, bf16[96,3,8192]{2,0,1:T(8,128)(2,1)}, u32[]{:S(2)}) %copy-start) | copy-done | bytes 4718616
  5.5 0.0 copy-start.4
  5.5 4.0 %cross_terms.1 = (bf16[288,4096]{1,0:T(8,128)(2,1)S(1)}, bf16[288,4096]{1,0:T(8,128)(2,1)}, bf16[16,4096]{1,0:T(8,128)(2,1)S(1)}, f32[8,304]{1,0:T(8,128)S(1)}) custom-call(s32[1]{0:T(128)} %bitcast.core_ref, bf16[288,8192]{1,0:T(8,128)(2,1)S(1)} %bitcast.10, f32[16,8192]{1,0:T(8,128)S(1)} %concatenate.3.mean_ref), custom_call_target="tpu_custom_call" | custom-call | flops 1207959552 | bytes 9437184 | tf_op jit(solution)/shard_map/cross_terms/pallas_call | solution.py:259
  9.6 0.0 copy-start.1
  9.6 0.7 copy-done.1
  10.2 8.8 %collective-permute-start = (bf16[288,4096]{1,0:T(8,128)(2,1)}, bf16[288,4096]{1,0:T(8,128)(2,1)}, u32[]{:S(2)}, u32[]{:S(2)}) collective-permute-start(bf16[288,4096]{1,0:T(8,128)(2,1)} %get-tuple-element.10), channel_id=1, source_target_pairs={{0,8},{8,0},{1,9},{9,1},{2,10},{10,2},{3,11},{11,3},{4,12},{12,4},... | collective-permute-start | bytes 7077896 | tf_op jit(solution)/shard_map/ppermute | solution.py:275
  19.1 10.2 %all_to_all.20.parts_ref = f32[16,8,304]{2,1,0:T(8,128)} all-to-all(f32[16,8,304]{2,1,0:T(8,128)S(1)} %broadcast_in_dim.29), channel_id=1, replica_groups=mesh['z'=8,'yh'=4,'core'=2,'yl'=2,'x'=4] {'core','yl','x'}, dimensions={0} | all-to-all | bytes 311296 | tf_op jit(solution)/shard_map/all_to_all | solution.py:276
  29.3 0.0 copy-done.4
  29.3 1.0 broadcast_in_dim.28
  30.3 11.6 %all-to-all-start = ((bf16[32,96,128]{2,1,0:T(8,128)(2,1)}), bf16[32,96,128]{2,1,0:T(8,128)(2,1)S(1)}, u32[]{:S(2)}, u32[]{:S(2)}) async-start(bf16[32,96,128]{2,1,0:T(8,128)(2,1)} %broadcast_in_dim.28), calls=%async_computation | async-start | bytes 1572864 | tf_op jit(solution)/shard_map/all_to_all | solution.py:251
  41.9 0.0 copy-start.3
  41.9 0.9 copy-done.3
  42.8 3.3 %rotation.1.rot_ref = f32[776,96]{1,0:T(8,128)S(1)} custom-call(s32[1]{0:T(128)} %bitcast.core_ref, f32[16,8,304]{2,1,0:T(8,128)S(1)} %copy-done.3), custom_call_target="tpu_custom_call" | custom-call | flops 1000000000 | bytes 1000000 | tf_op jit(solution)/shard_map/rotation/pallas_call | solution.py:279
  46.1 21.7 %all-to-all-done.vec_ref = bf16[32,96,128]{2,1,0:T(8,128)(2,1)S(1)} async-done(((bf16[32,96,128]{2,1,0:T(8,128)(2,1)}), bf16[32,96,128]{2,1,0:T(8,128)(2,1)S(1)}, u32[]{:S(2)}, u32[]{:S(2)}) %all-to-all-start) | async-done | bytes 786464 | tf_op jit(solution)/shard_map/all_to_all | solution.py:251
  67.8 0.0 collective-permute-done.recv_ref
  67.8 0.9 copy-done.2
  68.8 4.1 %projection.1 = f32[48,128]{1,0:T(8,128)S(1)} custom-call(s32[1]{0:T(128)} %bitcast.core_ref, bf16[288,4096]{1,0:T(8,128)(2,1)S(1)} %get-tuple-element.9.keep_ref, bf16[288,4096]{1,0:T(8,128)(2,1)} %collective-permute-done.recv_ref, bf16[16,4096]{1,0:T(8,128)(2,1)S(1)} %copy-done.2, bf16[32,96,128]{2,1,0:T(8,128)(2,1)S(1)} %all-to-all-done.vec_ref, ...), custom_call_target="tpu_custom_call" | custom-call | flops 1207959552 | bytes 4718592 | tf_op jit(solution)/shard_map/projection/pallas_call | solution.py:292
  72.9 13.4 %all_to_all.21.parts_ref = f32[16,48,128]{2,1,0:T(8,128)S(1)} all-to-all(f32[16,48,128]{2,1,0:T(8,128)S(1)} %broadcast_in_dim.30), channel_id=1, replica_groups=mesh['z'=8,'yh'=4,'core'=2,'yl'=2,'x'=4] {'core','yl','x'}, dimensions={0} | all-to-all | bytes 786432 | tf_op jit(solution)/shard_map/all_to_all | solution.py:303
  86.3 4.7 %product_terms.1 = bf16[32,96,128]{2,1,0:T(8,128)(2,1)S(1)} custom-call(s32[1]{0:T(128)} %bitcast.core_ref, f32[16,48,128]{2,1,0:T(8,128)S(1)} %all_to_all.21.parts_ref, f32[776,96]{1,0:T(8,128)S(1)} %rotation.1.rot_ref, bf16[288,4096]{1,0:T(8,128)(2,1)S(1)} %get-tuple-element.9.keep_ref, bf16[288,4096]{1,0:T(8,128)(2,1)} %collective-permute-done.recv_ref, ...), custom_call_target="tpu_custom_call" | custom-call | flops 1358954496 | bytes 4718592 | tf_op jit(solution)/shard_map/product_terms/pallas_call | solution.py:306
  91.0 31.1 %all_to_all.22 = bf16[32,96,128]{2,1,0:T(8,128)(2,1)S(1)} all-to-all(bf16[32,96,128]{2,1,0:T(8,128)(2,1)S(1)} %product_terms.1), channel_id=1, replica_groups=mesh['z'=8,'yh'=4,'core'=2,'yl'=2,'x'=4] {'z','yh'}, dimensions={0} | all-to-all | bytes 1572864 | tf_op jit(solution)/shard_map/all_to_all | solution.py:320
  122.1 0.1 convert_reduce_fusion
  122.2 0.6 broadcast_multiply_fusion
  (5 shorter events, 0.1 us)
Async XLA Ops:
  3.2 2.3 %copy-start = (bf16[96,3,8192]{2,0,1:T(8,128)(2,1)S(1)}, bf16[96,3,8192]{2,0,1:T(8,128)(2,1)}, u32[]{:S(2)}) copy-start(bf16[96,3,8192]{2,0,1:T(8,128)(2,1)} %param.3) | copy-start | bytes 14155780
  5.5 23.7 %copy-start.4 = (bf16[32,3,128]{2,0,1:T(8,128)(2,1)S(1)}, bf16[32,3,128]{2,0,1:T(8,128)(2,1)}, u32[]{:S(2)}) copy-start(bf16[32,3,128]{2,0,1:T(8,128)(2,1)} %param.5) | copy-start | bytes 73732
  9.6 0.7 copy-start.1
  10.2 57.6 %collective-permute-start = (bf16[288,4096]{1,0:T(8,128)(2,1)}, bf16[288,4096]{1,0:T(8,128)(2,1)}, u32[]{:S(2)}, u32[]{:S(2)}) collective-permute-start(bf16[288,4096]{1,0:T(8,128)(2,1)} %get-tuple-element.10), channel_id=1, source_target_pairs={{0,8},{8,0},{1,9},{9,1},{2,10},{10,2},{3,11},{11,3},{4,12},{12,4},... | collective-permute-start | bytes 7077896 | tf_op jit(solution)/shard_map/ppermute | solution.py:275
  30.3 37.6 %all-to-all-start = ((bf16[32,96,128]{2,1,0:T(8,128)(2,1)}), bf16[32,96,128]{2,1,0:T(8,128)(2,1)S(1)}, u32[]{:S(2)}, u32[]{:S(2)}) async-start(bf16[32,96,128]{2,1,0:T(8,128)(2,1)} %broadcast_in_dim.28), calls=%async_computation | async-start | bytes 1572864 | tf_op jit(solution)/shard_map/all_to_all | solution.py:251
  41.9 0.9 copy-start.3
  67.8 0.9 copy-start.2

commit v2 on v0

v2 whole, which is shorter than its diff:
```python
import functools

import jax
import jax.numpy as jnp
from jax import lax
from jax.experimental import pallas as pl
from jax.experimental.pallas import tpu as pltpu
from jax.sharding import Mesh
from jax.sharding import PartitionSpec as P

NS_STEPS = 8
LANES = 128
PAIR = 256
EXTRA = 16
F32 = jnp.float32
BF16 = jnp.bfloat16
HIGHEST = lax.Precision.HIGHEST
NT = (((1,), (1,)), ((), ()))
TN = (((0,), (0,)), ((), ()))


def iota(shape, dim):
    return lax.broadcasted_iota(jnp.int32, shape, dim)


def split3(value):
    high = value.astype(BF16)
    rest = value - high.astype(F32)
    middle = rest.astype(BF16)
    low = (rest - middle.astype(F32)).astype(BF16)
    return high, middle, low


def mean_rows(mean):
    shape = (EXTRA, mean.shape[1])
    row = iota(shape, 0)
    spread = jnp.where(row == 9, 1.0, 0.0)
    for i in range(3):
        spread = jnp.where((row < 9) & (row % 3 == i), mean[i : i + 1, :], spread)
    high, middle, low = split3(spread)
    take = jnp.where((row >= 3) & (row < 6), middle.astype(F32), jnp.where((row >= 6) & (row < 9), low.astype(F32), high.astype(F32)))
    return take.astype(BF16)


def cross_kernel(place_ref, x_ref, mean_ref, keep_ref, send_ref, rows_ref, cross_ref, acc_ref):
    step = pl.program_id(0)
    parity, core = place_ref[0], place_ref[1]
    extra = mean_rows(mean_ref[...])
    width = x_ref.shape[1]

    @pl.when(step == 0)
    def _():
        acc_ref[...] = jnp.zeros_like(acc_ref)

    total = acc_ref[...]
    pairs = width // PAIR
    for pair in range(pairs):
        columns = slice(pair * PAIR, (pair + 1) * PAIR)
        side = extra[:, columns]
        left = jnp.concatenate([x_ref[:, columns], side], axis=0)
        total += lax.dot_general(left, side, NT, preferred_element_type=F32)
        block = slice(pair % (pairs // 2) * LANES, (pair % (pairs // 2) + 1) * LANES)
        first, second = left[:, :LANES], left[:, LANES:]
        mine = jnp.where(core == 0, first, second)
        theirs = jnp.where(core == 0, second, first)
        other = (parity + pair // (pairs // 2)) % 2
        keep_ref[other, :, block] = mine[:-EXTRA]
        send_ref[other, :, block] = theirs[:-EXTRA]
        rows_ref[other, :, block] = mine[-EXTRA:]
    acc_ref[...] = total

    @pl.when(step == pl.num_programs(0) - 1)
    def _():
        row, col = iota((8, EXTRA), 0), iota((8, EXTRA), 1)
        pick = ((row < 3) & (col < 9) & ((col == row) | (col == row + 3) | (col == row + 6))) | ((row == 3) & (col == 9))
        cross = lax.dot_general(pick.astype(F32), total, NT, precision=HIGHEST, preferred_element_type=F32)
        cross_ref[...] = jnp.broadcast_to(cross[None], cross_ref.shape)


def polar_factor(amat):
    for _ in range(NS_STEPS):
        square = [[sum(amat[i][j] * amat[k][j] for j in range(3)) for k in range(3)] for i in range(3)]
        amat = [[1.5 * amat[i][j] - 0.5 * sum(square[i][k] * amat[k][j] for k in range(3)) for j in range(3)] for i in range(3)]
    return amat


def rotation_kernel(natom, core_ref, parts_ref, gram_ref, out_ref, proj_ref):
    half = parts_ref.shape[0] // 2
    frames = (parts_ref.shape[2] - EXTRA) // 3
    lanes = out_ref.shape[1]
    first, second = parts_ref[0], parts_ref[half]
    for index in range(1, half):
        first += parts_ref[index]
        second += parts_ref[half + index]
    is_first = core_ref[0] == 0
    own = jnp.where(is_first, first, second)
    other = jnp.where(is_first, second, first)
    ones_at = 3 * frames + 9
    centre = [own[i : i + 1, ones_at : ones_at + 1] / natom for i in range(3)]
    columns = [[total[:, j * frames : (j + 1) * frames] for total in (own, other)] for j in range(3)]
    row = lambda index, j: jnp.concatenate([part[index : index + 1] for part in columns[j]], axis=0)
    sums = [row(3, j) for j in range(3)]
    cross = [[row(i, j) - centre[i] * sums[j] for j in range(3)] for i in range(3)]
    scale = jnp.sqrt(1.0 + sum(cross[i][j] * cross[i][j] for i in range(3) for j in range(3)))
    rotation = polar_factor([[cross[i][j] / scale for j in range(3)] for i in range(3)])
    shift = [sum(rotation[i][j] * (sums[j] / natom) for j in range(3)) for i in range(3)]
    entries = [rotation[i][j] for i in range(3) for j in range(3)] + shift
    at = iota((EXTRA, frames), 0)
    index3, lane = iota((3 * EXTRA, 4 * LANES), 0) % EXTRA, iota((3 * EXTRA, 4 * LANES), 1)
    third = lanes // 3
    place, within = lane // LANES, lane % LANES
    which = within // third
    chosen = ((place < 3) & (index3 == 3 * which + place)) | ((place == 3) & (index3 == 9 + which))
    chosen = jnp.where(chosen & (which < 3), 1.0, 0.0).astype(BF16)
    for side in range(2):
        packed = jnp.zeros((EXTRA, frames), F32)
        for index, entry in enumerate(entries):
            packed = jnp.where(at == index, entry[side : side + 1], packed)
        pieces = jnp.concatenate([piece.astype(F32) for piece in split3(packed)], axis=0).astype(BF16)
        spread = lax.dot_general(pieces, chosen, TN, preferred_element_type=F32)
        for index in range(4):
            begin = (2 * index + side) * frames
            out_ref[begin : begin + frames, :] = spread[:, index * LANES : index * LANES + lanes]
    which8 = lane_part((8, lanes))
    out_ref[8 * frames : 8 * frames + 8, :] = jnp.where(which8 == 0, centre[0], jnp.where(which8 == 1, centre[1], centre[2]))
    proj = packed_projection(is_first, gram_ref, out_ref, frames)
    proj_ref[...] = jnp.broadcast_to(proj[None], proj_ref.shape)


def lane_part(shape):
    lane = iota(shape, 1)
    third = shape[1] // 3
    return (lane >= third).astype(jnp.int32) + (lane >= 2 * third).astype(jnp.int32)


def fetch(refs, buffers, sems, others, chunks):
    width = refs[0].shape[2] // chunks
    copies = []
    for index, other in enumerate(others):
        for chunk in range(chunks):
            columns = pl.ds(chunk * width, width)
            group = []
            for which, (ref, buffer) in enumerate(zip(refs, buffers)):
                copy = pltpu.make_async_copy(
                    ref.at[other, :, columns], buffer.at[index, :, columns], sems.at[which, index * chunks + chunk]
                )
                copy.start()
                group.append(copy)
            copies.append(group)
    return copies


def halves_kernel(same_ref, up_ref, down_ref):
    half = up_ref.shape[1]
    up_ref[...] = same_ref[:, :half]
    down_ref[...] = same_ref[:, half:]


def gram_kernel(keep_hbm, recv_hbm, rows_ref, same_ref, below_ref, above_ref, out_ref, keep_ref, recv_ref, sems):
    chunks = sems.shape[1] // 2
    copies = fetch((keep_hbm, recv_hbm), (keep_ref, recv_ref), sems, (0, 1), chunks)
    total = jnp.zeros(out_ref.shape, F32)
    pairs = same_ref.shape[0] // 2
    for other in range(2):
        for pair in range(pairs):
            if pair % (pairs // chunks) == 0:
                for copy in copies[other * chunks + pair // (pairs // chunks)]:
                    copy.wait()
            columns = slice(pair * PAIR, (pair + 1) * PAIR)
            left = jnp.concatenate([ref[other, :, columns] for ref in (keep_ref, recv_ref, rows_ref)], axis=0)
            ref, at = (same_ref, 2 * pair) if other == 0 else ((below_ref, above_ref)[pair % 2], pair // 2 * 2)
            right = jnp.concatenate([ref[at], ref[at + 1]], axis=1)
            total += lax.dot_general(left, right, NT, preferred_element_type=F32)
    out_ref[...] = total


def packed_projection(is_first, gram_ref, rot_ref, frames):
    lanes = gram_ref.shape[1]
    third = lanes // 3
    extra = gram_ref[6 * frames :, :]
    vec_sums = extra[9:10, :]
    centre = rot_ref[8 * frames : 8 * frames + 1, :]
    part = lane_part((1, lanes))
    along = [extra[i : i + 1] + extra[3 + i : 4 + i] + extra[6 + i : 7 + i] for i in range(3)]
    mean_term = jnp.where(part == 0, along[0], jnp.where(part == 1, along[1], along[2])) - centre * vec_sums
    halves = []
    for side in range(2):
        value = -rot_ref[(6 + side) * frames : (7 + side) * frames, :] * vec_sums - mean_term
        for j in range(3):
            spread = rot_ref[(2 * j + side) * frames : (2 * j + side + 1) * frames, :]
            begin = (3 * side + j) * frames
            value += spread * gram_ref[begin : begin + frames, :]
        halves.append(value)
    first = jnp.where(is_first, halves[0], halves[1])
    second = jnp.where(is_first, halves[1], halves[0])
    value = jnp.concatenate([first, second], axis=0)
    quarter = frames // 2
    row, col = iota((lanes, 4 * third), 0), iota((lanes, 4 * third), 1)
    packed = jnp.zeros((quarter, 4 * third), F32)
    pieces = split3(value)
    for q in range(4):
        fold = jnp.where((row % third == col % third) & (col // third == q), 1.0, 0.0).astype(BF16)
        for piece in pieces:
            packed += jnp.dot(piece[q * quarter : (q + 1) * quarter, :], fold, preferred_element_type=F32)
    return packed


def product_weights(is_first, parts_ref, rot_ref, weight_ref, frames, scale):
    lanes = rot_ref.shape[1]
    third = lanes // 3

    packed = parts_ref[0]
    for index in range(1, parts_ref.shape[0]):
        packed += parts_ref[index]
    packed = packed.astype(BF16)
    row, col = iota((4 * third, lanes), 0), iota((4 * third, lanes), 1)
    quarters = []
    for q in range(4):
        unfold = (row % third == col % third) & (row // third == q)
        quarters.append(jnp.dot(packed, unfold.astype(F32).astype(BF16), preferred_element_type=F32))
    first = jnp.concatenate(quarters[:2], axis=0)
    second = jnp.concatenate(quarters[2:], axis=0)
    sides = (jnp.where(is_first, first, second), jnp.where(is_first, second, first))
    centre = rot_ref[8 * frames : 8 * frames + 1, :]
    pieces = []
    proj_sum = jnp.zeros((1, lanes), F32)
    shift_sum = jnp.zeros((1, lanes), F32)
    for side in range(2):
        for j in range(3):
            begin = (2 * j + side) * frames
            pieces.append(rot_ref[begin : begin + frames, :] * sides[side])
        proj_sum += jnp.sum(sides[side], axis=0, keepdims=True)
        shift = rot_ref[(6 + side) * frames : (7 + side) * frames, :]
        shift_sum += jnp.sum(sides[side] * shift, axis=0, keepdims=True)
    at, part = iota((EXTRA, lanes), 0), lane_part((EXTRA, lanes))
    is_mean = (at < 9) & ((at == part) | (at == part + 3) | (at == part + 6))
    tail = jnp.where(is_mean, -proj_sum, jnp.where(at == 9, centre * proj_sum - shift_sum, 0.0))
    weight = jnp.concatenate(pieces + [tail], axis=0) * scale
    same = (iota((lanes, lanes), 0) == iota((lanes, lanes), 1)).astype(F32).astype(BF16)
    for index, piece in enumerate(split3(weight)):
        turned = lax.dot_general(same, piece, NT, preferred_element_type=F32)
        weight_ref[index * lanes : (index + 1) * lanes, :] = turned.astype(BF16)


def weighted(weight, refs, columns):
    term = jnp.dot(weight, jnp.concatenate([ref[0, :, columns] for ref in refs], axis=0), preferred_element_type=F32)
    lanes = term.shape[0] // 3
    return term[2 * lanes :] + term[lanes : 2 * lanes] + term[:lanes]


def product_kernel(
    scale, core_ref, parts_ref, rot_ref, keep_hbm, recv_hbm, rows_ref, up_ref, down_ref, weight_ref, keep_ref, recv_ref, sems
):
    chunks = sems.shape[1]
    copies = fetch((keep_hbm, recv_hbm), (keep_ref, recv_ref), sems, (1,), chunks)
    product_weights(core_ref[0] == 0, parts_ref, rot_ref, weight_ref, keep_ref.shape[1] // 3, scale)
    weight = weight_ref[...]
    pairs = up_ref.shape[0]
    for pair in range(pairs):
        if pair % (pairs // chunks) == 0:
            for copy in copies[pair // (pairs // chunks)]:
                copy.wait()
        columns = slice(pair * PAIR, (pair + 1) * PAIR)
        term = weighted(weight, (keep_ref, recv_ref, rows_ref.at[pl.ds(1, 1)]), columns).astype(BF16)
        out_ref = (up_ref, down_ref)[pair % 2]
        out_ref[pair // 2 * 2] = term[:, :LANES]
        out_ref[pair // 2 * 2 + 1] = term[:, LANES:]


def product_same_kernel(weight_ref, keep_ref, recv_ref, rows_ref, out_ref):
    weight = weight_ref[...]
    for pair in range(out_ref.shape[0] // 2):
        term = weighted(weight, (keep_ref, recv_ref, rows_ref), slice(pair * PAIR, (pair + 1) * PAIR))
        out_ref[2 * pair] = term[:, :LANES]
        out_ref[2 * pair + 1] = term[:, LANES:]


MIB = 1024 * 1024
GRAM_FLOPS = 10000000000
ROTATION_FLOPS = 10**9
HALVES_FLOPS = 20000000000
SMEM_SPEC = pl.BlockSpec(memory_space=pltpu.SMEM)


def params(limit=16):
    return pltpu.CompilerParams(vmem_limit_bytes=limit * MIB, dimension_semantics=("arbitrary",))


def cost(flops, moved):
    return pl.CostEstimate(flops=flops, bytes_accessed=moved, transcendentals=0)


def whole(*shape):
    return pl.BlockSpec(shape, lambda step: (0,) * len(shape))


def body(frames_xyz, mean_xyz, vector_block):
    frames, _, atoms = frames_xyz.shape
    kcount, _, own_atoms = vector_block.shape
    lanes = 3 * kcount
    rows = 3 * frames
    steps, quads = lax.axis_size("zh"), lax.axis_size("yh")
    chips = steps * quads
    peers = 2 * lax.axis_size("yl") * lax.axis_size("x")
    natom = atoms * lax.axis_size("yl") * lax.axis_size("x")
    frame_count = frames * 4 * chips
    ring = 2 * steps
    upward = [(i, (i + 1) % ring) for i in range(ring)]
    downward = [(i, (i - 1) % ring) for i in range(ring)]
    core = lax.axis_index("core").astype(jnp.int32).reshape(1)
    place = jnp.concatenate([lax.axis_index("zp").astype(jnp.int32).reshape(1), core])
    x_rows = frames_xyz.transpose(1, 0, 2).reshape(rows, atoms)
    vec_rows = vector_block.transpose(1, 0, 2).reshape(lanes, own_atoms)
    same = lax.all_to_all(
        jnp.broadcast_to(vec_rows[None], (chips, lanes, own_atoms)), ("zh", "yh"), 0, 0, tiled=True
    )

    wide, narrow = atoms // steps, atoms // steps // 4
    both = lambda height: pl.BlockSpec((2, height, narrow), lambda step: (0, 0, step))
    part = lambda height, which: pl.BlockSpec((1, height, narrow), lambda step: (which, 0, step))
    sorted_shape = lambda height: jax.ShapeDtypeStruct((2, height, steps * narrow), BF16)
    keep, send, side, cross = pl.pallas_call(
        cross_kernel,
        grid=(steps,),
        in_specs=[
            SMEM_SPEC,
            pl.BlockSpec((rows, wide), lambda step: (0, step)),
            pl.BlockSpec((3, wide), lambda step: (0, step)),
        ],
        out_specs=[both(rows), both(rows), both(EXTRA), whole(peers, 8, rows + EXTRA)],
        out_shape=[
            sorted_shape(rows), sorted_shape(rows), sorted_shape(EXTRA), jax.ShapeDtypeStruct((peers, 8, rows + EXTRA), F32),
        ],
        scratch_shapes=[pltpu.VMEM((rows + EXTRA, EXTRA), F32)],
        compiler_params=params(),
        cost_estimate=cost(2 * rows * atoms * 256, 4 * rows * atoms),
        name="cross_terms",
    )(place, x_rows, mean_xyz)
    recv = lax.ppermute(send, "core", [(0, 1), (1, 0)])
    cross, same = lax.optimization_barrier((cross, same))
    parts = lax.all_to_all(cross, ("core", "yl", "x"), 0, 0, tiled=True)
    shape = (chips // 2, lanes, own_atoms)
    vmem, hbm = pl.BlockSpec(memory_space=pltpu.VMEM), pl.BlockSpec(memory_space=pl.ANY)
    to_above, to_below = pl.pallas_call(
        halves_kernel,
        in_specs=[vmem],
        out_specs=[vmem, vmem],
        out_shape=[jax.ShapeDtypeStruct((steps, quads // 2, lanes, own_atoms), BF16)] * 2,
        compiler_params=pltpu.CompilerParams(vmem_limit_bytes=16 * MIB),
        cost_estimate=cost(HALVES_FLOPS, 10**6),
        name="vector_halves",
    )(same.reshape(steps, quads, lanes, own_atoms))
    below = lax.ppermute(to_above.reshape(shape), ("zh", "zp"), upward)
    above = lax.ppermute(to_below.reshape(shape), ("zh", "zp"), downward)
    blocks = lambda count: pl.BlockSpec((count, lanes, LANES), lambda step: (step, 0, 0))
    gram_rows = 2 * rows + EXTRA
    chunks = 2 if steps > 1 else 1
    gram = pl.pallas_call(
        gram_kernel,
        in_specs=[hbm, hbm, vmem, vmem, vmem, vmem],
        out_specs=vmem,
        out_shape=jax.ShapeDtypeStruct((gram_rows, lanes), F32),
        scratch_shapes=[pltpu.VMEM(keep.shape, BF16)] * 2 + [pltpu.SemaphoreType.DMA((2, 2 * chunks))],
        compiler_params=pltpu.CompilerParams(vmem_limit_bytes=16 * MIB),
        cost_estimate=cost(GRAM_FLOPS, 10**6),
        name="vector_products",
    )(keep, recv, side, same, below, above)
    rot_shape = (8 * frames + 8, lanes)
    rot, proj = pl.pallas_call(
        functools.partial(rotation_kernel, natom),
        in_specs=[SMEM_SPEC, vmem, vmem],
        out_specs=[vmem, vmem],
        out_shape=[
            jax.ShapeDtypeStruct(rot_shape, F32),
            jax.ShapeDtypeStruct((peers, frames // 2, 4 * kcount), F32),
        ],
        compiler_params=pltpu.CompilerParams(vmem_limit_bytes=16 * MIB),
        cost_estimate=cost(ROTATION_FLOPS, 10**6),
        name="rotation_projection",
    )(core, parts, gram)
    proj_parts = lax.all_to_all(proj, ("core", "yl", "x"), 0, 0, tiled=True)
    up, down, weight = pl.pallas_call(
        functools.partial(product_kernel, 1.0 / frame_count),
        in_specs=[SMEM_SPEC, vmem, vmem, hbm, hbm, vmem],
        out_specs=[vmem, vmem, vmem],
        out_shape=[
            jax.ShapeDtypeStruct(shape, BF16), jax.ShapeDtypeStruct(shape, BF16),
            jax.ShapeDtypeStruct((3 * lanes, gram_rows), BF16),
        ],
        scratch_shapes=[pltpu.VMEM((1, rows, steps * narrow), BF16)] * 2 + [pltpu.SemaphoreType.DMA((2, 2 * chunks))],
        compiler_params=pltpu.CompilerParams(vmem_limit_bytes=16 * MIB),
        cost_estimate=cost(1, 1),
        name="product_terms",
    )(core, proj_parts, rot, keep, recv, side)
    from_below = lax.ppermute(up, ("zh", "zp"), upward)
    from_above = lax.ppermute(down, ("zh", "zp"), downward)
    own = pl.pallas_call(
        product_same_kernel,
        grid=(steps,),
        in_specs=[whole(3 * lanes, gram_rows), part(rows, 0), part(rows, 0), part(EXTRA, 0)],
        out_specs=blocks(quads),
        out_shape=jax.ShapeDtypeStruct((chips, lanes, LANES), F32),
        compiler_params=params(),
        cost_estimate=cost(2 * rows * atoms * 256, 4 * rows * atoms),
        name="product_terms_same",
    )(weight, keep, recv, side)
    halves = (steps, quads // 2, lanes, own_atoms)
    neighbours = jnp.concatenate([from_below.reshape(halves), from_above.reshape(halves)], axis=1)
    term = (own + neighbours.reshape(own.shape).astype(F32)).astype(BF16)
    terms = lax.all_to_all(term, ("zh", "yh"), 0, 0, tiled=True)
    total = jnp.sum(terms.astype(F32), axis=0)
    return total.reshape(3, kcount, own_atoms).transpose(1, 0, 2)


def solution(mesh):
    inner = Mesh(mesh.devices.reshape(mesh_sizes(mesh)), ("zh", "zp", "yh", "core", "yl", "x"))
    frames, coords = ("zh", "zp", "yh", "core"), ("yl", "x")
    in_specs = (P(frames, None, coords), P(None, coords), P(None, None, coords + frames))
    out_specs = P(None, None, coords + frames)
    return jax.shard_map(body, mesh=inner, in_specs=in_specs, out_specs=out_specs, check_vma=False)


def mesh_sizes(mesh):
    frames, coords = mesh.shape["frames"], mesh.shape["coords"]
    return (frames // 16, 2, 4, 2, 2, coords // 2)
```

time: 721 us -> 109 us (0.15)
  waiting for transfers between devices: 580 us -> 10.7 us
  matrix products: 69.3 us -> 0 us
  starting transfers between devices: 0.04 us -> 37.7 us
  Pallas kernels: 0 us -> 18 us
  between operations: 14.1 us -> 0.14 us
  blocking collectives: 43.6 us -> 34.2 us
  other arithmetic: 8.64 us -> 0.89 us
    psum x1 -> x0, waiting for transfers between devices: 569 us -> none  [body(): summed = lax.psum(term, 'frames')]
    dot_general x20 -> x0, matrix products: 69.3 us -> none  [the longest x1 30.4 us: body(): jnp.einsum('ijf,fja->fia', rotation, shifted, precision=lax.Precision.HIG...]
    psum x2 -> x0, blocking collectives: 43.6 us -> none  [the longest x1 26.2 us: body(): projection = lax.psum(partial_proj, 'coords').astype(jnp.bfloat16)]
    all_to_all x0 -> x2, blocking collectives: none -> 34.2 us  [the longest x1 21.8 us: body(): terms = lax.all_to_all(term, ('zh', 'yh'), 0, 0, tiled=True)]
    all_to_all x0 -> x2, starting transfers between devices: none -> 23.1 us  [the longest x1 16.2 us: body(): lax.all_to_all(jnp.broadcast_to(vec_rows[None], (chips, lanes, own_atoms)...]
    pallas_call x0 -> x6, Pallas kernels: none -> 18 us  [the longest x1 4.58 us: body(): pl.pallas_call(cross_kernel, grid=(steps,), in_specs=[SMEM_SPEC, pl.Block...]
    ppermute x0 -> x5, starting transfers between devices: none -> 14.6 us  [the longest x1 3.4 us: body(): above = lax.ppermute(to_below.reshape(shape), ('zh', 'zp'), downward)]
    all_gather x1 -> x0, waiting for transfers between devices: 10 us -> none  [body(): lax.all_gather(vector_block, 'frames', axis=2, tiled=True)]
  transfers between devices with their start and end apart: 2 -> 7, of which waited for: 2 -> 3; matrix products, arithmetic and copies ran while one was open for 8% -> 0% of each run, Pallas kernels for 0% -> 12%
where the time goes in v2:
time: 109 us; the launch traced here: 108 us
  starting transfers between devices  37.7 us (35%)
  blocking collectives  34.2 us (31%)
  Pallas kernels  18 us (17%)
  waiting for transfers between devices  10.7 us (10%)
  local copies, waits for them, and re-layouts  6.46 us (6%)
    all_to_all x1, blocking collectives, body(): terms = lax.all_to_all(term, ('zh', 'yh'), 0, 0, tiled=True)  21.8 us
    all_to_all x1, starting transfers between devices, body(): lax.all_to_all(jnp.broadcast_to(vec_rows[None], (chips, lanes, own_atoms)...  16.2 us
    all_to_all x1, blocking collectives, body(): proj_parts = lax.all_to_all(proj, ('core', 'yl', 'x'), 0, 0, tiled=True)  12.4 us
    all_to_all x1, starting transfers between devices, body(): parts = lax.all_to_all(cross, ('core', 'yl', 'x'), 0, 0, tiled=True)  6.89 us
    all_to_all x1, waiting for transfers between devices, body(): lax.all_to_all(jnp.broadcast_to(vec_rows[None], (chips, lanes, own_atoms)...  4.95 us
    unnamed x8, local copies, waits for them, and re-layouts  4.92 us
    pallas_call x1, Pallas kernels, body(): pl.pallas_call(cross_kernel, grid=(steps,), in_specs=[SMEM_SPEC, pl.Block...  4.58 us
    pallas_call x1, Pallas kernels, body(): pl.pallas_call(gram_kernel, in_specs=[hbm, hbm, vmem, vmem, vmem, vmem],...  4.01 us
  transfers between devices with their start and end apart: 7, of which 3 were waited for; matrix products, arithmetic and copies ran while one was open for 0% of the time, Pallas kernels for 12%

profile of v2, /device:TPU:1, one launch (start us, length us, event | category | flops | bytes accessed | tf_op | source)
XLA Modules:
  0.0 108.2 jit_solution(9798892181435295741)
XLA Ops:
  0.0 1.5 %broadcast_in_dim.8 = bf16[16,96,128]{2,1,0:T(8,128)(2,1)} broadcast(bf16[96,128]{1,0:T(8,128)(2,1)} %bitcast.23), dimensions={1,2} | broadcast | bytes 417792 | tf_op jit(solution)/shard_map/broadcast_in_dim | solution.py:315
  1.5 16.2 %all-to-all-start = ((bf16[16,96,128]{2,1,0:T(8,128)(2,1)}), bf16[16,96,128]{2,1,0:T(8,128)(2,1)S(1)}, u32[]{:S(2)}, u32[]{:S(2)}) async-start(bf16[16,96,128]{2,1,0:T(8,128)(2,1)} %broadcast_in_dim.8), calls=%async_computation | async-start | bytes 786432 | tf_op jit(solution)/shard_map/all_to_all | solution.py:314
  17.9 2.3 %copy-done = bf16[96,3,8192]{2,0,1:T(8,128)(2,1)S(1)} copy-done((bf16[96,3,8192]{2,0,1:T(8,128)(2,1)S(1)}, bf16[96,3,8192]{2,0,1:T(8,128)(2,1)}, u32[]{:S(2)}) %copy-start) | copy-done | bytes 4718616
  20.2 0.9 copy-done.1
  21.1 4.6 %cross_terms.1 = (bf16[2,288,2048]{2,1,0:T(8,128)(2,1)S(1)}, bf16[2,288,2048]{2,1,0:T(8,128)(2,1)}, bf16[2,16,2048]{2,1,0:T(8,128)(2,1)S(1)}, f32[16,8,304]{2,1,0:T(8,128)}) custom-call(s32[2]{0:T(128)S(1)} %pad_add_fusion.place_ref, bf16[288,8192]{1,0:T(8,128)(2,1)S(1)} %bitcast.19, f32[3,8192]{1,0:T(4,128)S(1)} %copy-done.1), custom_call_target="tpu_custom_call" | custom-call | flops 1207959552 | bytes 9437184 | tf_op jit(solution)/shard_map/cross_terms/pallas_call | solution.py:322
  25.7 2.9 %collective-permute-start = (bf16[2,288,2048]{2,1,0:T(8,128)(2,1)}, bf16[2,288,2048]{2,1,0:T(8,128)(2,1)}, u32[]{:S(2)}, u32[]{:S(2)}) collective-permute-start(bf16[2,288,2048]{2,1,0:T(8,128)(2,1)} %get-tuple-element.21), channel_id=1, source_target_pairs={{0,8},{8,0},{1,9},{9,1},{2,10},{10,2},{3,11},{11,3},{4,12},{12,4},... | collective-permute-start | bytes 7077896 | tf_op jit(solution)/shard_map/ppermute | solution.py:339
  28.5 5.0 %all-to-all-done.same_ref = bf16[16,96,128]{2,1,0:T(8,128)(2,1)S(1)} async-done(((bf16[16,96,128]{2,1,0:T(8,128)(2,1)}), bf16[16,96,128]{2,1,0:T(8,128)(2,1)S(1)}, u32[]{:S(2)}, u32[]{:S(2)}) %all-to-all-start) | async-done | bytes 393248 | tf_op jit(solution)/shard_map/all_to_all | solution.py:314
  33.5 0.8 vector_halves.1
  34.3 3.1 %collective-permute-start.1 = (bf16[8,96,128]{2,1,0:T(8,128)(2,1)}, bf16[8,96,128]{2,1,0:T(8,128)(2,1)S(1)}, u32[]{:S(2)}, u32[]{:S(2)}) collective-permute-start(bf16[8,96,128]{2,1,0:T(8,128)(2,1)} %bitcast.7), channel_id=1, source_target_pairs={{0,64},{64,128},{128,192},{192,256},{256,320},{320,384},{384,448},... | collective-permute-start | bytes 589832 | tf_op jit(solution)/shard_map/ppermute | solution.py:353
  37.4 3.4 %collective-permute-start.2 = (bf16[8,96,128]{2,1,0:T(8,128)(2,1)}, bf16[8,96,128]{2,1,0:T(8,128)(2,1)S(1)}, u32[]{:S(2)}, u32[]{:S(2)}) collective-permute-start(bf16[8,96,128]{2,1,0:T(8,128)(2,1)} %bitcast.8), channel_id=1, source_target_pairs={{0,448},{64,0},{128,64},{192,128},{256,192},{320,256},{384,320},{4... | collective-permute-start | bytes 589832 | tf_op jit(solution)/shard_map/ppermute | solution.py:354
  40.8 6.9 %all-to-all-start.1 = ((f32[16,8,304]{2,1,0:T(8,128)}), f32[16,8,304]{2,1,0:T(8,128)S(1)}, u32[]{:S(2)}, u32[]{:S(2)}) async-start(f32[16,8,304]{2,1,0:T(8,128)} %get-tuple-element.19), calls=%async_computation.1 | async-start | bytes 393216 | tf_op jit(solution)/shard_map/all_to_all | solution.py:341
  47.7 4.0 %vector_products.1.gram_ref = f32[592,96]{1,0:T(8,128)S(1)} custom-call(bf16[2,288,2048]{2,1,0:T(8,128)(2,1)S(1)} %get-tuple-element.20.keep_hbm.keep_ref, bf16[2,288,2048]{2,1,0:T(8,128)(2,1)} %collective-permute-done.recv_hbm.recv_ref, bf16[2,16,2048]{2,1,0:T(8,128)(2,1)S(1)} %get-tuple-element.22.rows_ref, ...), custom_call_target="tpu_custom_call" | custom-call | flops 10000000000 | bytes 1000000 | tf_op jit(solution)/shard_map/vector_products/pallas_call | solution.py:358
  51.7 0.7 copy-done.2
  52.4 2.3 %all-to-all-done.1.parts_ref = f32[16,8,304]{2,1,0:T(8,128)S(1)} async-done(((f32[16,8,304]{2,1,0:T(8,128)}), f32[16,8,304]{2,1,0:T(8,128)S(1)}, u32[]{:S(2)}, u32[]{:S(2)}) %all-to-all-start.1) | async-done | bytes 155680 | tf_op jit(solution)/shard_map/all_to_all | solution.py:341
  54.7 1.0 copy-done.3
  55.7 2.8 %rotation_projection.1 = (f32[776,96]{1,0:T(8,128)S(1)}, f32[16,48,128]{2,1,0:T(8,128)S(1)}) custom-call(s32[1]{0:T(128)} %bitcast.core_ref, f32[16,8,304]{2,1,0:T(8,128)S(1)} %all-to-all-done.1.parts_ref, f32[592,96]{1,0:T(8,128)S(1)} %copy-done.3), custom_call_target="tpu_custom_call" | custom-call | flops 1000000000 | bytes 1000000 | tf_op jit(solution)/shard_map/rotation_projection/pallas_call | solution.py:369
  58.4 12.4 %all_to_all.20.parts_ref = f32[16,48,128]{2,1,0:T(8,128)S(1)} all-to-all(f32[16,48,128]{2,1,0:T(8,128)S(1)} %get-tuple-element.26), channel_id=1, replica_groups=mesh['zh'=4,'zp'=2,'yh'=4,'core'=2,'yl'=2,'x'=4] {'core','yl','x'}, dimensions={0} | all-to-all | bytes 786432 | tf_op jit(solution)/shard_map/all_to_all | solution.py:381
  70.8 2.7 %product_terms.1 = (bf16[8,96,128]{2,1,0:T(8,128)(2,1)S(1)}, bf16[8,96,128]{2,1,0:T(8,128)(2,1)S(1)}, bf16[288,592]{1,0:T(8,128)(2,1)S(1)}) custom-call(s32[1]{0:T(128)} %bitcast.core_ref, f32[16,48,128]{2,1,0:T(8,128)S(1)} %all_to_all.20.parts_ref, f32[776,96]{1,0:T(8,128)S(1)} %get-tuple-element.27.rot_ref, ...), custom_call_target="tpu_custom_call" | custom-call | flops 1 | bytes 1 | tf_op jit(solution)/shard_map/product_terms/pallas_call | solution.py:382
  73.5 2.9 %collective-permute-start.4 = (bf16[8,96,128]{2,1,0:T(8,128)(2,1)S(1)}, bf16[8,96,128]{2,1,0:T(8,128)(2,1)S(1)}, u32[]{:S(2)}, u32[]{:S(2)}) collective-permute-start(bf16[8,96,128]{2,1,0:T(8,128)(2,1)S(1)} %get-tuple-element.30), channel_id=1, source_target_pairs={{0,448},{64,0},{128,64},{192,128},{256,192},{320,256},{384,320},{4... | collective-permute-start | bytes 589832 | tf_op jit(solution)/shard_map/ppermute | solution.py:396
  76.4 2.3 %collective-permute-start.3 = (bf16[8,96,128]{2,1,0:T(8,128)(2,1)S(1)}, bf16[8,96,128]{2,1,0:T(8,128)(2,1)S(1)}, u32[]{:S(2)}, u32[]{:S(2)}) collective-permute-start(bf16[8,96,128]{2,1,0:T(8,128)(2,1)S(1)} %get-tuple-element.29), channel_id=1, source_target_pairs={{0,64},{64,128},{128,192},{192,256},{256,320},{320,384},{384,448},... | collective-permute-start | bytes 589832 | tf_op jit(solution)/shard_map/ppermute | solution.py:395
  78.8 3.2 %product_terms_same.1 = f32[16,96,128]{2,1,0:T(8,128)S(1)} custom-call(bf16[288,592]{1,0:T(8,128)(2,1)S(1)} %get-tuple-element.28.weight_ref, bf16[2,288,2048]{2,1,0:T(8,128)(2,1)S(1)} %get-tuple-element.20.keep_hbm.keep_ref, bf16[2,288,2048]{2,1,0:T(8,128)(2,1)} %collective-permute-done.recv_hbm.recv_ref, bf16[2,16,2048]{2,1,0:T(8,128)(2,1)S(1)} %get-tuple-element.22.rows_ref), custom_call_target="tpu_custom_call" | custom-call | flops 1207959552 | bytes 9437184 | tf_op jit(solution)/shard_map/product_terms_same/pallas_call | solution.py:397
  82.1 3.5 %collective-permute-done.3 = bf16[8,96,128]{2,1,0:T(8,128)(2,1)S(1)} collective-permute-done((bf16[8,96,128]{2,1,0:T(8,128)(2,1)S(1)}, bf16[8,96,128]{2,1,0:T(8,128)(2,1)S(1)}, u32[]{:S(2)}, u32[]{:S(2)}) %collective-permute-start.3) | collective-permute-done | bytes 196640 | tf_op jit(solution)/shard_map/ppermute | solution.py:395
  85.7 21.8 %all_to_all.21 = bf16[16,96,128]{2,1,0:T(8,128)(2,1)S(1)} all-to-all(bf16[16,96,128]{2,1,0:T(8,128)(2,1)S(1)} %fusion), channel_id=1, replica_groups=mesh['zh'=4,'zp'=2,'yh'=4,'core'=2,'yl'=2,'x'=4] {'zh','yh'}, dimensions={0} | all-to-all | bytes 786432 | tf_op jit(solution)/shard_map/all_to_all | solution.py:410
  107.5 0.7 convert_reduce_fusion
  (11 shorter events, 0.2 us)
Async XLA Ops:
  1.5 31.9 %all-to-all-start = ((bf16[16,96,128]{2,1,0:T(8,128)(2,1)}), bf16[16,96,128]{2,1,0:T(8,128)(2,1)S(1)}, u32[]{:S(2)}, u32[]{:S(2)}) async-start(bf16[16,96,128]{2,1,0:T(8,128)(2,1)} %broadcast_in_dim.8), calls=%async_computation | async-start | bytes 786432 | tf_op jit(solution)/shard_map/all_to_all | solution.py:314
  17.9 2.3 %copy-start = (bf16[96,3,8192]{2,0,1:T(8,128)(2,1)S(1)}, bf16[96,3,8192]{2,0,1:T(8,128)(2,1)}, u32[]{:S(2)}) copy-start(bf16[96,3,8192]{2,0,1:T(8,128)(2,1)} %param.3) | copy-start | bytes 14155780
  20.2 0.9 copy-start.1
  25.7 22.0 %collective-permute-start = (bf16[2,288,2048]{2,1,0:T(8,128)(2,1)}, bf16[2,288,2048]{2,1,0:T(8,128)(2,1)}, u32[]{:S(2)}, u32[]{:S(2)}) collective-permute-start(bf16[2,288,2048]{2,1,0:T(8,128)(2,1)} %get-tuple-element.21), channel_id=1, source_target_pairs={{0,8},{8,0},{1,9},{9,1},{2,10},{10,2},{3,11},{11,3},{4,12},{12,4},... | collective-permute-start | bytes 7077896 | tf_op jit(solution)/shard_map/ppermute | solution.py:339
  34.3 13.4 %collective-permute-start.1 = (bf16[8,96,128]{2,1,0:T(8,128)(2,1)}, bf16[8,96,128]{2,1,0:T(8,128)(2,1)S(1)}, u32[]{:S(2)}, u32[]{:S(2)}) collective-permute-start(bf16[8,96,128]{2,1,0:T(8,128)(2,1)} %bitcast.7), channel_id=1, source_target_pairs={{0,64},{64,128},{128,192},{192,256},{256,320},{320,384},{384,448},... | collective-permute-start | bytes 589832 | tf_op jit(solution)/shard_map/ppermute | solution.py:353
  37.4 10.3 %collective-permute-start.2 = (bf16[8,96,128]{2,1,0:T(8,128)(2,1)}, bf16[8,96,128]{2,1,0:T(8,128)(2,1)S(1)}, u32[]{:S(2)}, u32[]{:S(2)}) collective-permute-start(bf16[8,96,128]{2,1,0:T(8,128)(2,1)} %bitcast.8), channel_id=1, source_target_pairs={{0,448},{64,0},{128,64},{192,128},{256,192},{320,256},{384,320},{4... | collective-permute-start | bytes 589832 | tf_op jit(solution)/shard_map/ppermute | solution.py:354
  40.8 13.9 %all-to-all-start.1 = ((f32[16,8,304]{2,1,0:T(8,128)}), f32[16,8,304]{2,1,0:T(8,128)S(1)}, u32[]{:S(2)}, u32[]{:S(2)}) async-start(f32[16,8,304]{2,1,0:T(8,128)} %get-tuple-element.19), calls=%async_computation.1 | async-start | bytes 393216 | tf_op jit(solution)/shard_map/all_to_all | solution.py:341
  51.7 0.7 copy-start.2
  54.7 1.0 copy-start.3
  73.5 8.5 %collective-permute-start.4 = (bf16[8,96,128]{2,1,0:T(8,128)(2,1)S(1)}, bf16[8,96,128]{2,1,0:T(8,128)(2,1)S(1)}, u32[]{:S(2)}, u32[]{:S(2)}) collective-permute-start(bf16[8,96,128]{2,1,0:T(8,128)(2,1)S(1)} %get-tuple-element.30), channel_id=1, source_target_pairs={{0,448},{64,0},{128,64},{192,128},{256,192},{320,256},{384,320},{4... | collective-permute-start | bytes 589832 | tf_op jit(solution)/shard_map/ppermute | solution.py:396
  76.4 9.1 %collective-permute-start.3 = (bf16[8,96,128]{2,1,0:T(8,128)(2,1)S(1)}, bf16[8,96,128]{2,1,0:T(8,128)(2,1)S(1)}, u32[]{:S(2)}, u32[]{:S(2)}) collective-permute-start(bf16[8,96,128]{2,1,0:T(8,128)(2,1)S(1)} %get-tuple-element.29), channel_id=1, source_target_pairs={{0,64},{64,128},{128,192},{192,256},{256,320},{320,384},{384,448},... | collective-permute-start | bytes 589832 | tf_op jit(solution)/shard_map/ppermute | solution.py:395

commit v3 on v2

--- a/solution.py
+++ b/solution.py
@@ -150,27 +150,31 @@
     return copies
 
 
-def halves_kernel(same_ref, up_ref, down_ref):
-    half = up_ref.shape[1]
-    up_ref[...] = same_ref[:, :half]
-    down_ref[...] = same_ref[:, half:]
-
-
-def gram_kernel(keep_hbm, recv_hbm, rows_ref, same_ref, below_ref, above_ref, out_ref, keep_ref, recv_ref, sems):
-    chunks = sems.shape[1] // 2
-    copies = fetch((keep_hbm, recv_hbm), (keep_ref, recv_ref), sems, (0, 1), chunks)
-    total = jnp.zeros(out_ref.shape, F32)
-    pairs = same_ref.shape[0] // 2
-    for other in range(2):
-        for pair in range(pairs):
-            if pair % (pairs // chunks) == 0:
-                for copy in copies[other * chunks + pair // (pairs // chunks)]:
-                    copy.wait()
-            columns = slice(pair * PAIR, (pair + 1) * PAIR)
-            left = jnp.concatenate([ref[other, :, columns] for ref in (keep_ref, recv_ref, rows_ref)], axis=0)
-            ref, at = (same_ref, 2 * pair) if other == 0 else ((below_ref, above_ref)[pair % 2], pair // 2 * 2)
-            right = jnp.concatenate([ref[at], ref[at + 1]], axis=1)
-            total += lax.dot_general(left, right, NT, preferred_element_type=F32)
+def copies_kernel(vec_ref, out_ref, sems):
+    copies = [pltpu.make_async_copy(vec_ref, out_ref.at[index], sems.at[index]) for index in range(out_ref.shape[0])]
+    for copy in copies:
+        copy.start()
+    for copy in copies:
+        copy.wait()
+
+
+def pass_kernel(core_ref, after_ref, out_ref):
+    out_ref[0] = core_ref[0]
+
+
+def gram_kernel(other, keep_hbm, recv_hbm, rows_ref, vec_ref, *rest):
+    before, (out_ref, keep_ref, recv_ref, sems) = rest[:-4], rest[-4:]
+    copies = fetch((keep_hbm, recv_hbm), (keep_ref, recv_ref), sems, (other,), sems.shape[1])
+    total = before[0][...] if before else jnp.zeros(out_ref.shape, F32)
+    chunks, pairs = len(copies), vec_ref.shape[0] // 2
+    for pair in range(pairs):
+        if pair % (pairs // chunks) == 0:
+            for copy in copies[pair // (pairs // chunks)]:
+                copy.wait()
+        columns = slice(pair * PAIR, (pair + 1) * PAIR)
+        left = jnp.concatenate([keep_ref[0, :, columns], recv_ref[0, :, columns], rows_ref[other, :, columns]], axis=0)
+        right = jnp.concatenate([vec_ref[2 * pair], vec_ref[2 * pair + 1]], axis=1)
+        total += lax.dot_general(left, right, NT, preferred_element_type=F32)
     out_ref[...] = total
 
 
@@ -276,9 +280,10 @@
 
 
 MIB = 1024 * 1024
-GRAM_FLOPS = 10000000000
+GRAM_LIMIT = 16
+GRAM_FLOPS = 1
 ROTATION_FLOPS = 10**9
-HALVES_FLOPS = 20000000000
+PASS_FLOPS = 40000000000
 SMEM_SPEC = pl.BlockSpec(memory_space=pltpu.SMEM)
 
 
@@ -311,10 +316,19 @@
     place = jnp.concatenate([lax.axis_index("zp").astype(jnp.int32).reshape(1), core])
     x_rows = frames_xyz.transpose(1, 0, 2).reshape(rows, atoms)
     vec_rows = vector_block.transpose(1, 0, 2).reshape(lanes, own_atoms)
-    same = lax.all_to_all(
-        jnp.broadcast_to(vec_rows[None], (chips, lanes, own_atoms)), ("zh", "yh"), 0, 0, tiled=True
-    )
-
+    vmem, hbm = pl.BlockSpec(memory_space=pltpu.VMEM), pl.BlockSpec(memory_space=pl.ANY)
+    limits = pltpu.CompilerParams(vmem_limit_bytes=16 * MIB)
+    copies = pl.pallas_call(
+        copies_kernel,
+        in_specs=[hbm],
+        out_specs=hbm,
+        out_shape=jax.ShapeDtypeStruct((chips, lanes, own_atoms), BF16),
+        scratch_shapes=[pltpu.SemaphoreType.DMA((chips,))],
+        compiler_params=limits,
+        cost_estimate=cost(1, 1),
+        name="vector_copies",
+    )(vec_rows)
+    same = lax.all_to_all(copies, ("zh", "yh"), 0, 0, tiled=True)
     wide, narrow = atoms // steps, atoms // steps // 4
     both = lambda height: pl.BlockSpec((2, height, narrow), lambda step: (0, 0, step))
     part = lambda height, which: pl.BlockSpec((1, height, narrow), lambda step: (which, 0, step))
@@ -337,34 +351,36 @@
         name="cross_terms",
     )(place, x_rows, mean_xyz)
     recv = lax.ppermute(send, "core", [(0, 1), (1, 0)])
-    cross, same = lax.optimization_barrier((cross, same))
+    core_after = pl.pallas_call(
+        pass_kernel,
+        in_specs=[SMEM_SPEC, hbm],
+        out_specs=SMEM_SPEC,
+        out_shape=jax.ShapeDtypeStruct((1,), jnp.int32),
+        cost_estimate=cost(PASS_FLOPS, 10**6),
+        name="pass_core",
+    )(core, cross)
+    cross, core_after, same = lax.optimization_barrier((cross, core_after, same))
+    opposite = lax.ppermute(same, ("zh", "zp"), downward)
     parts = lax.all_to_all(cross, ("core", "yl", "x"), 0, 0, tiled=True)
-    shape = (chips // 2, lanes, own_atoms)
-    vmem, hbm = pl.BlockSpec(memory_space=pltpu.VMEM), pl.BlockSpec(memory_space=pl.ANY)
-    to_above, to_below = pl.pallas_call(
-        halves_kernel,
-        in_specs=[vmem],
-        out_specs=[vmem, vmem],
-        out_shape=[jax.ShapeDtypeStruct((steps, quads // 2, lanes, own_atoms), BF16)] * 2,
-        compiler_params=pltpu.CompilerParams(vmem_limit_bytes=16 * MIB),
-        cost_estimate=cost(HALVES_FLOPS, 10**6),
-        name="vector_halves",
-    )(same.reshape(steps, quads, lanes, own_atoms))
-    below = lax.ppermute(to_above.reshape(shape), ("zh", "zp"), upward)
-    above = lax.ppermute(to_below.reshape(shape), ("zh", "zp"), downward)
     blocks = lambda count: pl.BlockSpec((count, lanes, LANES), lambda step: (step, 0, 0))
     gram_rows = 2 * rows + EXTRA
     chunks = 2 if steps > 1 else 1
-    gram = pl.pallas_call(
-        gram_kernel,
-        in_specs=[hbm, hbm, vmem, vmem, vmem, vmem],
-        out_specs=vmem,
-        out_shape=jax.ShapeDtypeStruct((gram_rows, lanes), F32),
-        scratch_shapes=[pltpu.VMEM(keep.shape, BF16)] * 2 + [pltpu.SemaphoreType.DMA((2, 2 * chunks))],
-        compiler_params=pltpu.CompilerParams(vmem_limit_bytes=16 * MIB),
-        cost_estimate=cost(GRAM_FLOPS, 10**6),
-        name="vector_products",
-    )(keep, recv, side, same, below, above)
+    fetched = [pltpu.VMEM((1, rows, steps * narrow), BF16)] * 2 + [pltpu.SemaphoreType.DMA((2, chunks))]
+    def products(other, vec, *before):
+        return pl.pallas_call(
+            functools.partial(gram_kernel, other),
+            in_specs=[hbm, hbm, vmem, vmem] + [vmem] * len(before),
+            out_specs=vmem,
+            out_shape=jax.ShapeDtypeStruct((gram_rows, lanes), F32),
+            scratch_shapes=[
+                *fetched,
+            ],
+            compiler_params=pltpu.CompilerParams(vmem_limit_bytes=GRAM_LIMIT * MIB),
+            cost_estimate=cost(GRAM_FLOPS, 10**6),
+            name="vector_products",
+        )(keep, recv, side, vec, *before)
+
+    gram = products(1, opposite, products(0, same))
     rot_shape = (8 * frames + 8, lanes)
     rot, proj = pl.pallas_call(
         functools.partial(rotation_kernel, natom),
@@ -374,24 +390,26 @@
             jax.ShapeDtypeStruct(rot_shape, F32),
             jax.ShapeDtypeStruct((peers, frames // 2, 4 * kcount), F32),
         ],
-        compiler_params=pltpu.CompilerParams(vmem_limit_bytes=16 * MIB),
+        compiler_params=limits,
         cost_estimate=cost(ROTATION_FLOPS, 10**6),
         name="rotation_projection",
-    )(core, parts, gram)
+    )(core_after, parts, gram)
     proj_parts = lax.all_to_all(proj, ("core", "yl", "x"), 0, 0, tiled=True)
     up, down, weight = pl.pallas_call(
         functools.partial(product_kernel, 1.0 / frame_count),
         in_specs=[SMEM_SPEC, vmem, vmem, hbm, hbm, vmem],
         out_specs=[vmem, vmem, vmem],
         out_shape=[
-            jax.ShapeDtypeStruct(shape, BF16), jax.ShapeDtypeStruct(shape, BF16),
+            jax.ShapeDtypeStruct((chips // 2, lanes, own_atoms), BF16),
+            jax.ShapeDtypeStruct((chips // 2, lanes, own_atoms), BF16),
             jax.ShapeDtypeStruct((3 * lanes, gram_rows), BF16),
         ],
-        scratch_shapes=[pltpu.VMEM((1, rows, steps * narrow), BF16)] * 2 + [pltpu.SemaphoreType.DMA((2, 2 * chunks))],
-        compiler_params=pltpu.CompilerParams(vmem_limit_bytes=16 * MIB),
+        scratch_shapes=fetched,
+        compiler_params=limits,
         cost_estimate=cost(1, 1),
         name="product_terms",
     )(core, proj_parts, rot, keep, recv, side)
+    shape = (chips // 2, lanes, own_atoms)
     from_below = lax.ppermute(up, ("zh", "zp"), upward)
     from_above = lax.ppermute(down, ("zh", "zp"), downward)
     own = pl.pallas_call(

time: 109 us -> 104 us (0.954)
  waiting for transfers between devices: 10.7 us -> 6.64 us
  local copies, waits for them, and re-layouts: 6.46 us -> 3.98 us
  Pallas kernels: 18 us -> 20.3 us
  starting transfers between devices: 37.7 us -> 36.2 us
    ppermute x1, waiting for transfers between devices: 3.48 us -> 0.01 us  [body(): from_below = lax.ppermute(up, ('zh', 'zp'), upward)]
    ppermute x2 -> x1, starting transfers between devices: 6.48 us -> 3.98 us  [body(): opposite = lax.ppermute(same, ('zh', 'zp'), downward)]
    pallas_call x2 -> x4, Pallas kernels: 4.79 us -> 6.76 us  [the longest x2 5.34 us: products(): pl.pallas_call(functools.partial(gram_kernel, other), in_specs=[hbm, hbm,...]
    ppermute x1, starting transfers between devices: 2.93 us -> 4.57 us  [body(): from_above = lax.ppermute(down, ('zh', 'zp'), downward)]
    broadcast_in_dim x1 -> x0, local copies, waits for them, and re-layouts: 1.54 us -> none  [body(): jnp.broadcast_to(vec_rows[None], (chips, lanes, own_atoms))]
    unnamed x8 -> x6, local copies, waits for them, and re-layouts: 4.92 us -> 3.98 us
  transfers between devices with their start and end apart: 7 -> 6, of which waited for: 3 -> 3; matrix products, arithmetic and copies ran while one was open for 0% -> 0% of each run, Pallas kernels for 12% -> 13%
where the time goes in v3:
time: 104 us; the launch traced here: 103 us
  starting transfers between devices  36.2 us (35%)
  blocking collectives  35.2 us (34%)
  Pallas kernels  20.3 us (20%)
  waiting for transfers between devices  6.64 us (6%)
  local copies, waits for them, and re-layouts  3.98 us (4%)
    all_to_all x1, blocking collectives, body(): terms = lax.all_to_all(term, ('zh', 'yh'), 0, 0, tiled=True)  22.2 us
    all_to_all x1, starting transfers between devices, body(): same = lax.all_to_all(copies, ('zh', 'yh'), 0, 0, tiled=True)  16.2 us
    all_to_all x1, blocking collectives, body(): proj_parts = lax.all_to_all(proj, ('core', 'yl', 'x'), 0, 0, tiled=True)  13 us
    all_to_all x1, starting transfers between devices, body(): parts = lax.all_to_all(cross, ('core', 'yl', 'x'), 0, 0, tiled=True)  6.6 us
    pallas_call x2, Pallas kernels, products(): pl.pallas_call(functools.partial(gram_kernel, other), in_specs=[hbm, hbm,...  5.34 us
    ppermute x1, starting transfers between devices, body(): from_above = lax.ppermute(down, ('zh', 'zp'), downward)  4.57 us
    pallas_call x1, Pallas kernels, body(): pl.pallas_call(cross_kernel, grid=(steps,), in_specs=[SMEM_SPEC, pl.Block...  4.54 us
    all_to_all x1, waiting for transfers between devices, body(): same = lax.all_to_all(copies, ('zh', 'yh'), 0, 0, tiled=True)  4.46 us
  transfers between devices with their start and end apart: 6, of which 3 were waited for; matrix products, arithmetic and copies ran while one was open for 0% of the time, Pallas kernels for 13%

profile of v3, /device:TPU:1, one launch (start us, length us, event | category | flops | bytes accessed | tf_op | source)
XLA Modules:
  0.0 103.3 jit_solution(14045708295833757417)
XLA Ops:
  0.0 0.7 copy-done.2
  0.7 0.9 vector_copies.1
  1.6 16.2 %all-to-all-start = ((bf16[16,96,128]{2,1,0:T(8,128)(2,1)}), bf16[16,96,128]{2,1,0:T(8,128)(2,1)S(1)}, u32[]{:S(2)}, u32[]{:S(2)}) async-start(bf16[16,96,128]{2,1,0:T(8,128)(2,1)} %vector_copies.1), calls=%async_computation | async-start | bytes 786432 | tf_op jit(solution)/shard_map/all_to_all | solution.py:331
  18.0 2.3 %copy-done = bf16[96,3,8192]{2,0,1:T(8,128)(2,1)S(1)} copy-done((bf16[96,3,8192]{2,0,1:T(8,128)(2,1)S(1)}, bf16[96,3,8192]{2,0,1:T(8,128)(2,1)}, u32[]{:S(2)}) %copy-start) | copy-done | bytes 4718616
  20.3 0.9 copy-done.1
  21.2 4.5 %cross_terms.1 = (bf16[2,288,2048]{2,1,0:T(8,128)(2,1)S(1)}, bf16[2,288,2048]{2,1,0:T(8,128)(2,1)}, bf16[2,16,2048]{2,1,0:T(8,128)(2,1)S(1)}, f32[16,8,304]{2,1,0:T(8,128)}) custom-call(s32[2]{0:T(128)S(1)} %pad_add_fusion.place_ref, bf16[288,8192]{1,0:T(8,128)(2,1)S(1)} %bitcast.16, f32[3,8192]{1,0:T(4,128)S(1)} %copy-done.1), custom_call_target="tpu_custom_call" | custom-call | flops 1207959552 | bytes 9437184 | tf_op jit(solution)/shard_map/cross_terms/pallas_call | solution.py:336
  25.8 2.9 %collective-permute-start = (bf16[2,288,2048]{2,1,0:T(8,128)(2,1)}, bf16[2,288,2048]{2,1,0:T(8,128)(2,1)}, u32[]{:S(2)}, u32[]{:S(2)}) collective-permute-start(bf16[2,288,2048]{2,1,0:T(8,128)(2,1)} %get-tuple-element.21), channel_id=1, source_target_pairs={{0,8},{8,0},{1,9},{9,1},{2,10},{10,2},{3,11},{11,3},{4,12},{12,4},... | collective-permute-start | bytes 7077896 | tf_op jit(solution)/shard_map/ppermute | solution.py:353
  28.6 0.5 pass_core.1.core_ref
  29.1 4.5 %all-to-all-done.vec_ref = bf16[16,96,128]{2,1,0:T(8,128)(2,1)S(1)} async-done(((bf16[16,96,128]{2,1,0:T(8,128)(2,1)}), bf16[16,96,128]{2,1,0:T(8,128)(2,1)S(1)}, u32[]{:S(2)}, u32[]{:S(2)}) %all-to-all-start) | async-done | bytes 393248 | tf_op jit(solution)/shard_map/all_to_all | solution.py:331
  33.6 4.0 %collective-permute-start.1 = (bf16[16,96,128]{2,1,0:T(8,128)(2,1)S(1)}, bf16[16,96,128]{2,1,0:T(8,128)(2,1)S(1)}, u32[]{:S(2)}, u32[]{:S(2)}) collective-permute-start(bf16[16,96,128]{2,1,0:T(8,128)(2,1)S(1)} %all-to-all-done.vec_ref), channel_id=1, source_target_pairs={{0,448},{64,0},{128,64},{192,128},{256,192},{320,256},{384,320},{4... | collective-permute-start | bytes 1179656 | tf_op jit(solution)/shard_map/ppermute | solution.py:363
  37.6 6.6 %all-to-all-start.1 = ((f32[16,8,304]{2,1,0:T(8,128)}), f32[16,8,304]{2,1,0:T(8,128)S(1)}, u32[]{:S(2)}, u32[]{:S(2)}) async-start(f32[16,8,304]{2,1,0:T(8,128)} %get-tuple-element.19.after_ref), calls=%async_computation.1 | async-start | bytes 393216 | tf_op jit(solution)/shard_map/all_to_all | solution.py:364
  44.2 2.7 %vector_products.2.rest_0_ = f32[592,96]{1,0:T(8,128)S(1)} custom-call(bf16[2,288,2048]{2,1,0:T(8,128)(2,1)S(1)} %get-tuple-element.20.keep_hbm.keep_ref, bf16[2,288,2048]{2,1,0:T(8,128)(2,1)} %collective-permute-done.recv_hbm.recv_ref, bf16[2,16,2048]{2,1,0:T(8,128)(2,1)S(1)} %get-tuple-element.22.rows_ref, bf16[16,96,128]{2,1,0:T(8,128)(2,1)S(1)} %all-to-all-done.vec_ref), custom_call_target="tpu_custom_call" | custom-call | flops 1 | bytes 1000000 | tf_op jit(solution)/shard_map/vector_products/pallas_call | solution.py:370
  46.9 2.7 %vector_products.3.gram_ref = f32[592,96]{1,0:T(8,128)S(1)} custom-call(bf16[2,288,2048]{2,1,0:T(8,128)(2,1)S(1)} %get-tuple-element.20.keep_hbm.keep_ref, bf16[2,288,2048]{2,1,0:T(8,128)(2,1)} %collective-permute-done.recv_hbm.recv_ref, bf16[2,16,2048]{2,1,0:T(8,128)(2,1)S(1)} %get-tuple-element.22.rows_ref, ...), custom_call_target="tpu_custom_call" | custom-call | flops 1 | bytes 1000000 | tf_op jit(solution)/shard_map/vector_products/pallas_call | solution.py:370
  49.6 1.7 %all-to-all-done.1.parts_ref = f32[16,8,304]{2,1,0:T(8,128)S(1)} async-done(((f32[16,8,304]{2,1,0:T(8,128)}), f32[16,8,304]{2,1,0:T(8,128)S(1)}, u32[]{:S(2)}, u32[]{:S(2)}) %all-to-all-start.1) | async-done | bytes 155680 | tf_op jit(solution)/shard_map/all_to_all | solution.py:364
  51.2 3.3 %rotation_projection.1 = (f32[776,96]{1,0:T(8,128)S(1)}, f32[16,48,128]{2,1,0:T(8,128)S(1)}) custom-call(s32[1]{0:T(128)} %pass_core.1.core_ref, f32[16,8,304]{2,1,0:T(8,128)S(1)} %all-to-all-done.1.parts_ref, f32[592,96]{1,0:T(8,128)S(1)} %vector_products.3.gram_ref), custom_call_target="tpu_custom_call" | custom-call | flops 1000000000 | bytes 1000000 | tf_op jit(solution)/shard_map/rotation_projection/pallas_call | solution.py:385
  54.6 13.0 %all_to_all.20.parts_ref = f32[16,48,128]{2,1,0:T(8,128)S(1)} all-to-all(f32[16,48,128]{2,1,0:T(8,128)S(1)} %get-tuple-element.24), channel_id=1, replica_groups=mesh['zh'=4,'zp'=2,'yh'=4,'core'=2,'yl'=2,'x'=4] {'core','yl','x'}, dimensions={0} | all-to-all | bytes 786432 | tf_op jit(solution)/shard_map/all_to_all | solution.py:397
  67.6 2.4 %product_terms.1 = (bf16[8,96,128]{2,1,0:T(8,128)(2,1)S(1)}, bf16[8,96,128]{2,1,0:T(8,128)(2,1)S(1)}, bf16[288,592]{1,0:T(8,128)(2,1)S(1)}) custom-call(s32[1]{0:T(128)} %bitcast.core_ref, f32[16,48,128]{2,1,0:T(8,128)S(1)} %all_to_all.20.parts_ref, f32[776,96]{1,0:T(8,128)S(1)} %get-tuple-element.25.rot_ref, ...), custom_call_target="tpu_custom_call" | custom-call | flops 1 | bytes 1 | tf_op jit(solution)/shard_map/product_terms/pallas_call | solution.py:398
  70.0 1.9 %collective-permute-start.2 = (bf16[8,96,128]{2,1,0:T(8,128)(2,1)S(1)}, bf16[8,96,128]{2,1,0:T(8,128)(2,1)S(1)}, u32[]{:S(2)}, u32[]{:S(2)}) collective-permute-start(bf16[8,96,128]{2,1,0:T(8,128)(2,1)S(1)} %get-tuple-element.27), channel_id=1, source_target_pairs={{0,64},{64,128},{128,192},{192,256},{256,320},{320,384},{384,448},... | collective-permute-start | bytes 589832 | tf_op jit(solution)/shard_map/ppermute | solution.py:413
  71.9 4.6 %collective-permute-start.3 = (bf16[8,96,128]{2,1,0:T(8,128)(2,1)S(1)}, bf16[8,96,128]{2,1,0:T(8,128)(2,1)S(1)}, u32[]{:S(2)}, u32[]{:S(2)}) collective-permute-start(bf16[8,96,128]{2,1,0:T(8,128)(2,1)S(1)} %get-tuple-element.28), channel_id=1, source_target_pairs={{0,448},{64,0},{128,64},{192,128},{256,192},{320,256},{384,320},{4... | collective-permute-start | bytes 589832 | tf_op jit(solution)/shard_map/ppermute | solution.py:414
  76.5 3.2 %product_terms_same.1 = f32[16,96,128]{2,1,0:T(8,128)S(1)} custom-call(bf16[288,592]{1,0:T(8,128)(2,1)S(1)} %get-tuple-element.26.weight_ref, bf16[2,288,2048]{2,1,0:T(8,128)(2,1)S(1)} %get-tuple-element.20.keep_hbm.keep_ref, bf16[2,288,2048]{2,1,0:T(8,128)(2,1)} %collective-permute-done.recv_hbm.recv_ref, bf16[2,16,2048]{2,1,0:T(8,128)(2,1)S(1)} %get-tuple-element.22.rows_ref), custom_call_target="tpu_custom_call" | custom-call | flops 1207959552 | bytes 9437184 | tf_op jit(solution)/shard_map/product_terms_same/pallas_call | solution.py:415
  79.7 0.5 collective-permute-done.3
  80.3 0.1 fusion
  80.4 22.2 %all_to_all.21 = bf16[16,96,128]{2,1,0:T(8,128)(2,1)S(1)} all-to-all(bf16[16,96,128]{2,1,0:T(8,128)(2,1)S(1)} %fusion), channel_id=1, replica_groups=mesh['zh'=4,'zp'=2,'yh'=4,'core'=2,'yl'=2,'x'=4] {'zh','yh'}, dimensions={0} | all-to-all | bytes 786432 | tf_op jit(solution)/shard_map/all_to_all | solution.py:428
  102.6 0.7 convert_reduce_fusion
  (8 shorter events, 0.1 us)
Async XLA Ops:
  0.0 0.7 copy-start.2
  1.6 32.0 %all-to-all-start = ((bf16[16,96,128]{2,1,0:T(8,128)(2,1)}), bf16[16,96,128]{2,1,0:T(8,128)(2,1)S(1)}, u32[]{:S(2)}, u32[]{:S(2)}) async-start(bf16[16,96,128]{2,1,0:T(8,128)(2,1)} %vector_copies.1), calls=%async_computation | async-start | bytes 786432 | tf_op jit(solution)/shard_map/all_to_all | solution.py:331
  18.0 2.3 %copy-start = (bf16[96,3,8192]{2,0,1:T(8,128)(2,1)S(1)}, bf16[96,3,8192]{2,0,1:T(8,128)(2,1)}, u32[]{:S(2)}) copy-start(bf16[96,3,8192]{2,0,1:T(8,128)(2,1)} %param.3) | copy-start | bytes 14155780
  20.3 0.9 copy-start.1
  25.8 18.4 %collective-permute-start = (bf16[2,288,2048]{2,1,0:T(8,128)(2,1)}, bf16[2,288,2048]{2,1,0:T(8,128)(2,1)}, u32[]{:S(2)}, u32[]{:S(2)}) collective-permute-start(bf16[2,288,2048]{2,1,0:T(8,128)(2,1)} %get-tuple-element.21), channel_id=1, source_target_pairs={{0,8},{8,0},{1,9},{9,1},{2,10},{10,2},{3,11},{11,3},{4,12},{12,4},... | collective-permute-start | bytes 7077896 | tf_op jit(solution)/shard_map/ppermute | solution.py:353
  33.6 13.3 %collective-permute-start.1 = (bf16[16,96,128]{2,1,0:T(8,128)(2,1)S(1)}, bf16[16,96,128]{2,1,0:T(8,128)(2,1)S(1)}, u32[]{:S(2)}, u32[]{:S(2)}) collective-permute-start(bf16[16,96,128]{2,1,0:T(8,128)(2,1)S(1)} %all-to-all-done.vec_ref), channel_id=1, source_target_pairs={{0,448},{64,0},{128,64},{192,128},{256,192},{320,256},{384,320},{4... | collective-permute-start | bytes 1179656 | tf_op jit(solution)/shard_map/ppermute | solution.py:363
  37.6 13.6 %all-to-all-start.1 = ((f32[16,8,304]{2,1,0:T(8,128)}), f32[16,8,304]{2,1,0:T(8,128)S(1)}, u32[]{:S(2)}, u32[]{:S(2)}) async-start(f32[16,8,304]{2,1,0:T(8,128)} %get-tuple-element.19.after_ref), calls=%async_computation.1 | async-start | bytes 393216 | tf_op jit(solution)/shard_map/all_to_all | solution.py:364
  70.0 9.8 %collective-permute-start.2 = (bf16[8,96,128]{2,1,0:T(8,128)(2,1)S(1)}, bf16[8,96,128]{2,1,0:T(8,128)(2,1)S(1)}, u32[]{:S(2)}, u32[]{:S(2)}) collective-permute-start(bf16[8,96,128]{2,1,0:T(8,128)(2,1)S(1)} %get-tuple-element.27), channel_id=1, source_target_pairs={{0,64},{64,128},{128,192},{192,256},{256,320},{320,384},{384,448},... | collective-permute-start | bytes 589832 | tf_op jit(solution)/shard_map/ppermute | solution.py:413
  71.9 8.3 %collective-permute-start.3 = (bf16[8,96,128]{2,1,0:T(8,128)(2,1)S(1)}, bf16[8,96,128]{2,1,0:T(8,128)(2,1)S(1)}, u32[]{:S(2)}, u32[]{:S(2)}) collective-permute-start(bf16[8,96,128]{2,1,0:T(8,128)(2,1)S(1)} %get-tuple-element.28), channel_id=1, source_target_pairs={{0,448},{64,0},{128,64},{192,128},{256,192},{320,256},{384,320},{4... | collective-permute-start | bytes 589832 | tf_op jit(solution)/shard_map/ppermute | solution.py:414

commit v4 on v3

--- a/solution.py
+++ b/solution.py
@@ -124,7 +124,7 @@
     which8 = lane_part((8, lanes))
     out_ref[8 * frames : 8 * frames + 8, :] = jnp.where(which8 == 0, centre[0], jnp.where(which8 == 1, centre[1], centre[2]))
     proj = packed_projection(is_first, gram_ref, out_ref, frames)
-    proj_ref[...] = jnp.broadcast_to(proj[None], proj_ref.shape)
+    proj_ref[...] = jnp.broadcast_to(proj.astype(BF16)[None], proj_ref.shape)
 
 
 def lane_part(shape):
@@ -162,7 +162,11 @@
     out_ref[0] = core_ref[0]
 
 
-def gram_kernel(other, keep_hbm, recv_hbm, rows_ref, vec_ref, *rest):
+def by_yh(at, quads, pairs):
+    return at % quads * (2 * pairs // quads) + at // quads
+
+
+def gram_kernel(quads, other, keep_hbm, recv_hbm, rows_ref, vec_ref, *rest):
     before, (out_ref, keep_ref, recv_ref, sems) = rest[:-4], rest[-4:]
     copies = fetch((keep_hbm, recv_hbm), (keep_ref, recv_ref), sems, (other,), sems.shape[1])
     total = before[0][...] if before else jnp.zeros(out_ref.shape, F32)
@@ -173,7 +177,7 @@
                 copy.wait()
         columns = slice(pair * PAIR, (pair + 1) * PAIR)
         left = jnp.concatenate([keep_ref[0, :, columns], recv_ref[0, :, columns], rows_ref[other, :, columns]], axis=0)
-        right = jnp.concatenate([vec_ref[2 * pair], vec_ref[2 * pair + 1]], axis=1)
+        right = jnp.concatenate([vec_ref[by_yh(at, quads, pairs)] for at in (2 * pair, 2 * pair + 1)], axis=1)
         total += lax.dot_general(left, right, NT, preferred_element_type=F32)
     out_ref[...] = total
 
@@ -213,9 +217,9 @@
     lanes = rot_ref.shape[1]
     third = lanes // 3
 
-    packed = parts_ref[0]
+    packed = parts_ref[0].astype(F32)
     for index in range(1, parts_ref.shape[0]):
-        packed += parts_ref[index]
+        packed += parts_ref[index].astype(F32)
     packed = packed.astype(BF16)
     row, col = iota((4 * third, lanes), 0), iota((4 * third, lanes), 1)
     quarters = []
@@ -253,7 +257,7 @@
 
 
 def product_kernel(
-    scale, core_ref, parts_ref, rot_ref, keep_hbm, recv_hbm, rows_ref, up_ref, down_ref, weight_ref, keep_ref, recv_ref, sems
+    scale, quads, core_ref, parts_ref, rot_ref, keep_hbm, recv_hbm, rows_ref, up_ref, down_ref, weight_ref, keep_ref, recv_ref, sems
 ):
     chunks = sems.shape[1]
     copies = fetch((keep_hbm, recv_hbm), (keep_ref, recv_ref), sems, (1,), chunks)
@@ -266,17 +270,17 @@
                 copy.wait()
         columns = slice(pair * PAIR, (pair + 1) * PAIR)
         term = weighted(weight, (keep_ref, recv_ref, rows_ref.at[pl.ds(1, 1)]), columns).astype(BF16)
-        out_ref = (up_ref, down_ref)[pair % 2]
-        out_ref[pair // 2 * 2] = term[:, :LANES]
-        out_ref[pair // 2 * 2 + 1] = term[:, LANES:]
+        for index in range(2):
+            at = by_yh(2 * pair + index, quads, pairs)
+            (up_ref if at < pairs else down_ref)[at % pairs] = term[:, index * LANES : (index + 1) * LANES]
 
 
 def product_same_kernel(weight_ref, keep_ref, recv_ref, rows_ref, out_ref):
     weight = weight_ref[...]
     for pair in range(out_ref.shape[0] // 2):
         term = weighted(weight, (keep_ref, recv_ref, rows_ref), slice(pair * PAIR, (pair + 1) * PAIR))
-        out_ref[2 * pair] = term[:, :LANES]
-        out_ref[2 * pair + 1] = term[:, LANES:]
+        out_ref[2 * pair, 0] = term[:, :LANES]
+        out_ref[2 * pair + 1, 0] = term[:, LANES:]
 
 
 MIB = 1024 * 1024
@@ -328,7 +332,7 @@
         cost_estimate=cost(1, 1),
         name="vector_copies",
     )(vec_rows)
-    same = lax.all_to_all(copies, ("zh", "yh"), 0, 0, tiled=True)
+    same = lax.all_to_all(copies, ("yh", "zh"), 0, 0, tiled=True)
     wide, narrow = atoms // steps, atoms // steps // 4
     both = lambda height: pl.BlockSpec((2, height, narrow), lambda step: (0, 0, step))
     part = lambda height, which: pl.BlockSpec((1, height, narrow), lambda step: (which, 0, step))
@@ -368,7 +372,7 @@
     fetched = [pltpu.VMEM((1, rows, steps * narrow), BF16)] * 2 + [pltpu.SemaphoreType.DMA((2, chunks))]
     def products(other, vec, *before):
         return pl.pallas_call(
-            functools.partial(gram_kernel, other),
+            functools.partial(gram_kernel, quads, other),
             in_specs=[hbm, hbm, vmem, vmem] + [vmem] * len(before),
             out_specs=vmem,
             out_shape=jax.ShapeDtypeStruct((gram_rows, lanes), F32),
@@ -388,7 +392,7 @@
         out_specs=[vmem, vmem],
         out_shape=[
             jax.ShapeDtypeStruct(rot_shape, F32),
-            jax.ShapeDtypeStruct((peers, frames // 2, 4 * kcount), F32),
+            jax.ShapeDtypeStruct((peers, frames // 2, 4 * kcount), BF16),
         ],
         compiler_params=limits,
         cost_estimate=cost(ROTATION_FLOPS, 10**6),
@@ -396,7 +400,7 @@
     )(core_after, parts, gram)
     proj_parts = lax.all_to_all(proj, ("core", "yl", "x"), 0, 0, tiled=True)
     up, down, weight = pl.pallas_call(
-        functools.partial(product_kernel, 1.0 / frame_count),
+        functools.partial(product_kernel, 1.0 / frame_count, quads),
         in_specs=[SMEM_SPEC, vmem, vmem, hbm, hbm, vmem],
         out_specs=[vmem, vmem, vmem],
         out_shape=[
@@ -416,16 +420,15 @@
         product_same_kernel,
         grid=(steps,),
         in_specs=[whole(3 * lanes, gram_rows), part(rows, 0), part(rows, 0), part(EXTRA, 0)],
-        out_specs=blocks(quads),
-        out_shape=jax.ShapeDtypeStruct((chips, lanes, LANES), F32),
+        out_specs=pl.BlockSpec((quads, 1, lanes, LANES), lambda step: (0, step, 0, 0)),
+        out_shape=jax.ShapeDtypeStruct((quads, steps, lanes, LANES), F32),
         compiler_params=params(),
         cost_estimate=cost(2 * rows * atoms * 256, 4 * rows * atoms),
         name="product_terms_same",
     )(weight, keep, recv, side)
-    halves = (steps, quads // 2, lanes, own_atoms)
-    neighbours = jnp.concatenate([from_below.reshape(halves), from_above.reshape(halves)], axis=1)
-    term = (own + neighbours.reshape(own.shape).astype(F32)).astype(BF16)
-    terms = lax.all_to_all(term, ("zh", "yh"), 0, 0, tiled=True)
+    neighbours = jnp.concatenate([from_below, from_above], axis=0)
+    term = (own.reshape(neighbours.shape) + neighbours.astype(F32)).astype(BF16)
+    terms = lax.all_to_all(term, ("yh", "zh"), 0, 0, tiled=True)
     total = jnp.sum(terms.astype(F32), axis=0)
     return total.reshape(3, kcount, own_atoms).transpose(1, 0, 2)
 

time: 104 us -> 102 us (0.981); the launches traced: 103 us -> 100 us
  blocking collectives: 35.2 us -> 31.8 us
  waiting for transfers between devices: 6.64 us -> 8.5 us
  starting transfers between devices: 36.2 us -> 34.7 us
    all_to_all x1, blocking collectives: 13 us -> 11.1 us  [body(): proj_parts = lax.all_to_all(proj, ('core', 'yl', 'x'), 0, 0, tiled=True)]
    all_to_all x1, blocking collectives: 22.2 us -> 20.7 us  [body(): terms = lax.all_to_all(term, ('yh', 'zh'), 0, 0, tiled=True)]
    ppermute x1, starting transfers between devices: 4.57 us -> 3.33 us  [body(): from_above = lax.ppermute(down, ('zh', 'zp'), downward)]
    ppermute x1, starting transfers between devices: 1.92 us -> 3.16 us  [body(): from_below = lax.ppermute(up, ('zh', 'zp'), upward)]
    ppermute x1, starting transfers between devices: 3.98 us -> 2.76 us  [body(): opposite = lax.ppermute(same, ('zh', 'zp'), downward)]
    all_to_all x1, waiting for transfers between devices: 4.46 us -> 5.62 us  [body(): same = lax.all_to_all(copies, ('yh', 'zh'), 0, 0, tiled=True)]
  transfers between devices with their start and end apart: 6 -> 6, of which waited for: 3 -> 3; matrix products, arithmetic and copies ran while one was open for 0% -> 0% of each run, Pallas kernels for 13% -> 14%
where the time goes in v4:
time: 102 us; the launch traced here: 100 us
  starting transfers between devices  34.7 us (34%)
  blocking collectives  31.8 us (31%)
  Pallas kernels  20.3 us (20%)
  waiting for transfers between devices  8.5 us (8%)
  local copies, waits for them, and re-layouts  3.98 us (4%)
    all_to_all x1, blocking collectives, body(): terms = lax.all_to_all(term, ('yh', 'zh'), 0, 0, tiled=True)  20.7 us
    all_to_all x1, starting transfers between devices, body(): same = lax.all_to_all(copies, ('yh', 'zh'), 0, 0, tiled=True)  16.2 us
    all_to_all x1, blocking collectives, body(): proj_parts = lax.all_to_all(proj, ('core', 'yl', 'x'), 0, 0, tiled=True)  11.1 us
    all_to_all x1, starting transfers between devices, body(): parts = lax.all_to_all(cross, ('core', 'yl', 'x'), 0, 0, tiled=True)  6.32 us
    all_to_all x1, waiting for transfers between devices, body(): same = lax.all_to_all(copies, ('yh', 'zh'), 0, 0, tiled=True)  5.62 us
    pallas_call x2, Pallas kernels, products(): pl.pallas_call(functools.partial(gram_kernel, quads, other), in_specs=[hb...  5.34 us
    pallas_call x1, Pallas kernels, body(): pl.pallas_call(cross_kernel, grid=(steps,), in_specs=[SMEM_SPEC, pl.Block...  4.54 us
    unnamed x6, local copies, waits for them, and re-layouts  3.98 us
  transfers between devices with their start and end apart: 6, of which 3 were waited for; matrix products, arithmetic and copies ran while one was open for 0% of the time, Pallas kernels for 14%

profile of v4, /device:TPU:1, one launch (start us, length us, event | category | flops | bytes accessed | tf_op | source)
XLA Modules:
  0.0 100.2 jit_solution(9604092749868335719)
XLA Ops:
  0.0 0.7 copy-done.2
  0.7 0.9 vector_copies.1
  1.6 16.2 %all-to-all-start = ((bf16[16,96,128]{2,1,0:T(8,128)(2,1)}), bf16[16,96,128]{2,1,0:T(8,128)(2,1)S(1)}, u32[]{:S(2)}, u32[]{:S(2)}) async-start(bf16[16,96,128]{2,1,0:T(8,128)(2,1)} %vector_copies.1), calls=%async_computation | async-start | bytes 786432 | tf_op jit(solution)/shard_map/all_to_all | solution.py:335
  18.0 2.3 %copy-done = bf16[96,3,8192]{2,0,1:T(8,128)(2,1)S(1)} copy-done((bf16[96,3,8192]{2,0,1:T(8,128)(2,1)S(1)}, bf16[96,3,8192]{2,0,1:T(8,128)(2,1)}, u32[]{:S(2)}) %copy-start) | copy-done | bytes 4718616
  20.3 0.9 copy-done.1
  21.2 4.5 %cross_terms.1 = (bf16[2,288,2048]{2,1,0:T(8,128)(2,1)S(1)}, bf16[2,288,2048]{2,1,0:T(8,128)(2,1)}, bf16[2,16,2048]{2,1,0:T(8,128)(2,1)S(1)}, f32[16,8,304]{2,1,0:T(8,128)}) custom-call(s32[2]{0:T(128)S(1)} %pad_add_fusion.place_ref, bf16[288,8192]{1,0:T(8,128)(2,1)S(1)} %bitcast.15, f32[3,8192]{1,0:T(4,128)S(1)} %copy-done.1), custom_call_target="tpu_custom_call" | custom-call | flops 1207959552 | bytes 9437184 | tf_op jit(solution)/shard_map/cross_terms/pallas_call | solution.py:340
  25.8 2.9 %collective-permute-start = (bf16[2,288,2048]{2,1,0:T(8,128)(2,1)}, bf16[2,288,2048]{2,1,0:T(8,128)(2,1)}, u32[]{:S(2)}, u32[]{:S(2)}) collective-permute-start(bf16[2,288,2048]{2,1,0:T(8,128)(2,1)} %get-tuple-element.21), channel_id=1, source_target_pairs={{0,8},{8,0},{1,9},{9,1},{2,10},{10,2},{3,11},{11,3},{4,12},{12,4},... | collective-permute-start | bytes 7077896 | tf_op jit(solution)/shard_map/ppermute | solution.py:357
  28.6 0.5 pass_core.1.core_ref
  29.1 5.6 %all-to-all-done.vec_ref = bf16[16,96,128]{2,1,0:T(8,128)(2,1)S(1)} async-done(((bf16[16,96,128]{2,1,0:T(8,128)(2,1)}), bf16[16,96,128]{2,1,0:T(8,128)(2,1)S(1)}, u32[]{:S(2)}, u32[]{:S(2)}) %all-to-all-start) | async-done | bytes 393248 | tf_op jit(solution)/shard_map/all_to_all | solution.py:335
  34.8 2.8 %collective-permute-start.1 = (bf16[16,96,128]{2,1,0:T(8,128)(2,1)S(1)}, bf16[16,96,128]{2,1,0:T(8,128)(2,1)S(1)}, u32[]{:S(2)}, u32[]{:S(2)}) collective-permute-start(bf16[16,96,128]{2,1,0:T(8,128)(2,1)S(1)} %all-to-all-done.vec_ref), channel_id=1, source_target_pairs={{0,448},{64,0},{128,64},{192,128},{256,192},{320,256},{384,320},{4... | collective-permute-start | bytes 1179656 | tf_op jit(solution)/shard_map/ppermute | solution.py:367
  37.5 6.3 %all-to-all-start.1 = ((f32[16,8,304]{2,1,0:T(8,128)}), f32[16,8,304]{2,1,0:T(8,128)S(1)}, u32[]{:S(2)}, u32[]{:S(2)}) async-start(f32[16,8,304]{2,1,0:T(8,128)} %get-tuple-element.19.after_ref), calls=%async_computation.1 | async-start | bytes 393216 | tf_op jit(solution)/shard_map/all_to_all | solution.py:368
  43.9 2.7 %vector_products.2.rest_0_ = f32[592,96]{1,0:T(8,128)S(1)} custom-call(bf16[2,288,2048]{2,1,0:T(8,128)(2,1)S(1)} %get-tuple-element.20.keep_hbm.keep_ref, bf16[2,288,2048]{2,1,0:T(8,128)(2,1)} %collective-permute-done.recv_hbm.recv_ref, bf16[2,16,2048]{2,1,0:T(8,128)(2,1)S(1)} %get-tuple-element.22.rows_ref, bf16[16,96,128]{2,1,0:T(8,128)(2,1)S(1)} %all-to-all-done.vec_ref), custom_call_target="tpu_custom_call" | custom-call | flops 1 | bytes 1000000 | tf_op jit(solution)/shard_map/vector_products/pallas_call | solution.py:374
  46.5 2.7 %vector_products.3.gram_ref = f32[592,96]{1,0:T(8,128)S(1)} custom-call(bf16[2,288,2048]{2,1,0:T(8,128)(2,1)S(1)} %get-tuple-element.20.keep_hbm.keep_ref, bf16[2,288,2048]{2,1,0:T(8,128)(2,1)} %collective-permute-done.recv_hbm.recv_ref, bf16[2,16,2048]{2,1,0:T(8,128)(2,1)S(1)} %get-tuple-element.22.rows_ref, ...), custom_call_target="tpu_custom_call" | custom-call | flops 1 | bytes 1000000 | tf_op jit(solution)/shard_map/vector_products/pallas_call | solution.py:374
  49.2 1.7 %all-to-all-done.1.parts_ref = f32[16,8,304]{2,1,0:T(8,128)S(1)} async-done(((f32[16,8,304]{2,1,0:T(8,128)}), f32[16,8,304]{2,1,0:T(8,128)S(1)}, u32[]{:S(2)}, u32[]{:S(2)}) %all-to-all-start.1) | async-done | bytes 155680 | tf_op jit(solution)/shard_map/all_to_all | solution.py:368
  50.9 3.3 %rotation_projection.1 = (f32[776,96]{1,0:T(8,128)S(1)}, bf16[16,48,128]{2,1,0:T(8,128)(2,1)S(1)}) custom-call(s32[1]{0:T(128)} %pass_core.1.core_ref, f32[16,8,304]{2,1,0:T(8,128)S(1)} %all-to-all-done.1.parts_ref, f32[592,96]{1,0:T(8,128)S(1)} %vector_products.3.gram_ref), custom_call_target="tpu_custom_call" | custom-call | flops 1000000000 | bytes 1000000 | tf_op jit(solution)/shard_map/rotation_projection/pallas_call | solution.py:389
  54.2 11.1 %all_to_all.20.parts_ref = bf16[16,48,128]{2,1,0:T(8,128)(2,1)S(1)} all-to-all(bf16[16,48,128]{2,1,0:T(8,128)(2,1)S(1)} %get-tuple-element.24), channel_id=1, replica_groups=mesh['zh'=4,'zp'=2,'yh'=4,'core'=2,'yl'=2,'x'=4] {'core','yl','x'}, dimensions={0} | all-to-all | bytes 393216 | tf_op jit(solution)/shard_map/all_to_all | solution.py:401
  65.3 2.4 %product_terms.1 = (bf16[8,96,128]{2,1,0:T(8,128)(2,1)S(1)}, bf16[8,96,128]{2,1,0:T(8,128)(2,1)S(1)}, bf16[288,592]{1,0:T(8,128)(2,1)S(1)}) custom-call(s32[1]{0:T(128)} %bitcast.core_ref, bf16[16,48,128]{2,1,0:T(8,128)(2,1)S(1)} %all_to_all.20.parts_ref, f32[776,96]{1,0:T(8,128)S(1)} %get-tuple-element.25.rot_ref, ...), custom_call_target="tpu_custom_call" | custom-call | flops 1 | bytes 1 | tf_op jit(solution)/shard_map/product_terms/pallas_call | solution.py:402
  67.7 3.2 %collective-permute-start.2 = (bf16[8,96,128]{2,1,0:T(8,128)(2,1)S(1)}, bf16[8,96,128]{2,1,0:T(8,128)(2,1)S(1)}, u32[]{:S(2)}, u32[]{:S(2)}) collective-permute-start(bf16[8,96,128]{2,1,0:T(8,128)(2,1)S(1)} %get-tuple-element.27), channel_id=1, source_target_pairs={{0,64},{64,128},{128,192},{192,256},{256,320},{320,384},{384,448},... | collective-permute-start | bytes 589832 | tf_op jit(solution)/shard_map/ppermute | solution.py:417
  70.9 3.3 %collective-permute-start.3 = (bf16[8,96,128]{2,1,0:T(8,128)(2,1)S(1)}, bf16[8,96,128]{2,1,0:T(8,128)(2,1)S(1)}, u32[]{:S(2)}, u32[]{:S(2)}) collective-permute-start(bf16[8,96,128]{2,1,0:T(8,128)(2,1)S(1)} %get-tuple-element.28), channel_id=1, source_target_pairs={{0,448},{64,0},{128,64},{192,128},{256,192},{320,256},{384,320},{4... | collective-permute-start | bytes 589832 | tf_op jit(solution)/shard_map/ppermute | solution.py:418
  74.3 3.3 %product_terms_same.1 = f32[4,4,96,128]{3,2,1,0:T(8,128)S(1)} custom-call(bf16[288,592]{1,0:T(8,128)(2,1)S(1)} %get-tuple-element.26.weight_ref, bf16[2,288,2048]{2,1,0:T(8,128)(2,1)S(1)} %get-tuple-element.20.keep_hbm.keep_ref, bf16[2,288,2048]{2,1,0:T(8,128)(2,1)} %collective-permute-done.recv_hbm.recv_ref, bf16[2,16,2048]{2,1,0:T(8,128)(2,1)S(1)} %get-tuple-element.22.rows_ref), custom_call_target="tpu_custom_call" | custom-call | flops 1207959552 | bytes 9437184 | tf_op jit(solution)/shard_map/product_terms_same/pallas_call | solution.py:419
  77.6 1.2 %collective-permute-done.3 = bf16[8,96,128]{2,1,0:T(8,128)(2,1)S(1)} collective-permute-done((bf16[8,96,128]{2,1,0:T(8,128)(2,1)S(1)}, bf16[8,96,128]{2,1,0:T(8,128)(2,1)S(1)}, u32[]{:S(2)}, u32[]{:S(2)}) %collective-permute-start.3) | collective-permute-done | bytes 196640 | tf_op jit(solution)/shard_map/ppermute | solution.py:418
  78.8 0.1 fusion
  78.8 20.7 %all_to_all.21 = bf16[16,96,128]{2,1,0:T(8,128)(2,1)S(1)} all-to-all(bf16[16,96,128]{2,1,0:T(8,128)(2,1)S(1)} %fusion), channel_id=1, replica_groups=mesh['zh'=4,'zp'=2,'yh'=4,'core'=2,'yl'=2,'x'=4] {'yh','zh'}, dimensions={0} | all-to-all | bytes 786432 | tf_op jit(solution)/shard_map/all_to_all | solution.py:431
  99.5 0.7 convert_reduce_fusion
  (7 shorter events, 0.1 us)
Async XLA Ops:
  0.0 0.7 copy-start.2
  1.6 33.1 %all-to-all-start = ((bf16[16,96,128]{2,1,0:T(8,128)(2,1)}), bf16[16,96,128]{2,1,0:T(8,128)(2,1)S(1)}, u32[]{:S(2)}, u32[]{:S(2)}) async-start(bf16[16,96,128]{2,1,0:T(8,128)(2,1)} %vector_copies.1), calls=%async_computation | async-start | bytes 786432 | tf_op jit(solution)/shard_map/all_to_all | solution.py:335
  18.0 2.3 %copy-start = (bf16[96,3,8192]{2,0,1:T(8,128)(2,1)S(1)}, bf16[96,3,8192]{2,0,1:T(8,128)(2,1)}, u32[]{:S(2)}) copy-start(bf16[96,3,8192]{2,0,1:T(8,128)(2,1)} %param.3) | copy-start | bytes 14155780
  20.3 0.9 copy-start.1
  25.8 18.1 %collective-permute-start = (bf16[2,288,2048]{2,1,0:T(8,128)(2,1)}, bf16[2,288,2048]{2,1,0:T(8,128)(2,1)}, u32[]{:S(2)}, u32[]{:S(2)}) collective-permute-start(bf16[2,288,2048]{2,1,0:T(8,128)(2,1)} %get-tuple-element.21), channel_id=1, source_target_pairs={{0,8},{8,0},{1,9},{9,1},{2,10},{10,2},{3,11},{11,3},{4,12},{12,4},... | collective-permute-start | bytes 7077896 | tf_op jit(solution)/shard_map/ppermute | solution.py:357
  34.8 11.8 %collective-permute-start.1 = (bf16[16,96,128]{2,1,0:T(8,128)(2,1)S(1)}, bf16[16,96,128]{2,1,0:T(8,128)(2,1)S(1)}, u32[]{:S(2)}, u32[]{:S(2)}) collective-permute-start(bf16[16,96,128]{2,1,0:T(8,128)(2,1)S(1)} %all-to-all-done.vec_ref), channel_id=1, source_target_pairs={{0,448},{64,0},{128,64},{192,128},{256,192},{320,256},{384,320},{4... | collective-permute-start | bytes 1179656 | tf_op jit(solution)/shard_map/ppermute | solution.py:367
  37.5 13.4 %all-to-all-start.1 = ((f32[16,8,304]{2,1,0:T(8,128)}), f32[16,8,304]{2,1,0:T(8,128)S(1)}, u32[]{:S(2)}, u32[]{:S(2)}) async-start(f32[16,8,304]{2,1,0:T(8,128)} %get-tuple-element.19.after_ref), calls=%async_computation.1 | async-start | bytes 393216 | tf_op jit(solution)/shard_map/all_to_all | solution.py:368
  67.7 9.8 %collective-permute-start.2 = (bf16[8,96,128]{2,1,0:T(8,128)(2,1)S(1)}, bf16[8,96,128]{2,1,0:T(8,128)(2,1)S(1)}, u32[]{:S(2)}, u32[]{:S(2)}) collective-permute-start(bf16[8,96,128]{2,1,0:T(8,128)(2,1)S(1)} %get-tuple-element.27), channel_id=1, source_target_pairs={{0,64},{64,128},{128,192},{192,256},{256,320},{320,384},{384,448},... | collective-permute-start | bytes 589832 | tf_op jit(solution)/shard_map/ppermute | solution.py:417
  70.9 7.8 %collective-permute-start.3 = (bf16[8,96,128]{2,1,0:T(8,128)(2,1)S(1)}, bf16[8,96,128]{2,1,0:T(8,128)(2,1)S(1)}, u32[]{:S(2)}, u32[]{:S(2)}) collective-permute-start(bf16[8,96,128]{2,1,0:T(8,128)(2,1)S(1)} %get-tuple-element.28), channel_id=1, source_target_pairs={{0,448},{64,0},{128,64},{192,128},{256,192},{320,256},{384,320},{4... | collective-permute-start | bytes 589832 | tf_op jit(solution)/shard_map/ppermute | solution.py:418

commit v5 on v4

--- a/solution.py
+++ b/solution.py
@@ -263,7 +263,7 @@
     copies = fetch((keep_hbm, recv_hbm), (keep_ref, recv_ref), sems, (1,), chunks)
     product_weights(core_ref[0] == 0, parts_ref, rot_ref, weight_ref, keep_ref.shape[1] // 3, scale)
     weight = weight_ref[...]
-    pairs = up_ref.shape[0]
+    pairs = (up_ref.shape[0] + down_ref.shape[0]) // 2
     for pair in range(pairs):
         if pair % (pairs // chunks) == 0:
             for copy in copies[pair // (pairs // chunks)]:
@@ -272,18 +272,29 @@
         term = weighted(weight, (keep_ref, recv_ref, rows_ref.at[pl.ds(1, 1)]), columns).astype(BF16)
         for index in range(2):
             at = by_yh(2 * pair + index, quads, pairs)
-            (up_ref if at < pairs else down_ref)[at % pairs] = term[:, index * LANES : (index + 1) * LANES]
-
-
-def product_same_kernel(weight_ref, keep_ref, recv_ref, rows_ref, out_ref):
+            ref, at = (up_ref, at) if at < up_ref.shape[0] else (down_ref, at - up_ref.shape[0])
+            ref[at] = term[:, index * LANES : (index + 1) * LANES]
+
+
+def product_same_kernel(weight_ref, keep_hbm, recv_hbm, rows_ref, out_ref, keep_ref, recv_ref, sems):
+    chunks = sems.shape[1]
+    copies = fetch((keep_hbm, recv_hbm), (keep_ref, recv_ref), sems, (0,), chunks)
     weight = weight_ref[...]
-    for pair in range(out_ref.shape[0] // 2):
-        term = weighted(weight, (keep_ref, recv_ref, rows_ref), slice(pair * PAIR, (pair + 1) * PAIR))
-        out_ref[2 * pair, 0] = term[:, :LANES]
-        out_ref[2 * pair + 1, 0] = term[:, LANES:]
+    quads = out_ref.shape[0]
+    pairs = quads * out_ref.shape[1] // 2
+    for pair in range(pairs):
+        if pair % (pairs // chunks) == 0:
+            for copy in copies[pair // (pairs // chunks)]:
+                copy.wait()
+        columns = slice(pair * PAIR, (pair + 1) * PAIR)
+        term = weighted(weight, (keep_ref, recv_ref, rows_ref.at[pl.ds(0, 1)]), columns)
+        for index in range(2):
+            high, quad = divmod(2 * pair + index, quads)
+            out_ref[quad, high] = term[:, index * LANES : (index + 1) * LANES]
 
 
 MIB = 1024 * 1024
+UP_SHARE = 10
 GRAM_LIMIT = 16
 GRAM_FLOPS = 1
 ROTATION_FLOPS = 10**9
@@ -399,13 +410,14 @@
         name="rotation_projection",
     )(core_after, parts, gram)
     proj_parts = lax.all_to_all(proj, ("core", "yl", "x"), 0, 0, tiled=True)
+    ups = chips * UP_SHARE // 16
     up, down, weight = pl.pallas_call(
         functools.partial(product_kernel, 1.0 / frame_count, quads),
         in_specs=[SMEM_SPEC, vmem, vmem, hbm, hbm, vmem],
         out_specs=[vmem, vmem, vmem],
         out_shape=[
-            jax.ShapeDtypeStruct((chips // 2, lanes, own_atoms), BF16),
-            jax.ShapeDtypeStruct((chips // 2, lanes, own_atoms), BF16),
+            jax.ShapeDtypeStruct((ups, lanes, own_atoms), BF16),
+            jax.ShapeDtypeStruct((chips - ups, lanes, own_atoms), BF16),
             jax.ShapeDtypeStruct((3 * lanes, gram_rows), BF16),
         ],
         scratch_shapes=fetched,
@@ -413,16 +425,15 @@
         cost_estimate=cost(1, 1),
         name="product_terms",
     )(core, proj_parts, rot, keep, recv, side)
-    shape = (chips // 2, lanes, own_atoms)
     from_below = lax.ppermute(up, ("zh", "zp"), upward)
     from_above = lax.ppermute(down, ("zh", "zp"), downward)
     own = pl.pallas_call(
         product_same_kernel,
-        grid=(steps,),
-        in_specs=[whole(3 * lanes, gram_rows), part(rows, 0), part(rows, 0), part(EXTRA, 0)],
-        out_specs=pl.BlockSpec((quads, 1, lanes, LANES), lambda step: (0, step, 0, 0)),
+        in_specs=[vmem, hbm, hbm, vmem],
+        out_specs=vmem,
         out_shape=jax.ShapeDtypeStruct((quads, steps, lanes, LANES), F32),
-        compiler_params=params(),
+        scratch_shapes=fetched,
+        compiler_params=limits,
         cost_estimate=cost(2 * rows * atoms * 256, 4 * rows * atoms),
         name="product_terms_same",
     )(weight, keep, recv, side)

time: 102 us -> 101 us (level); the launches traced: 100 us -> 101 us
  transfers between devices with their start and end apart: 6 -> 6, of which waited for: 3 -> 4; matrix products, arithmetic and copies ran while one was open for 0% -> 0% of each run, Pallas kernels for 14% -> 13%
where the time goes in v5:
time: 101 us
  starting transfers between devices  34.7 us (34%)
  blocking collectives  32.8 us (32%)
  Pallas kernels  19.4 us (19%)
  waiting for transfers between devices  8.8 us (9%)
  local copies, waits for them, and re-layouts  3.98 us (4%)
    all_to_all x1, blocking collectives, body(): terms = lax.all_to_all(term, ('yh', 'zh'), 0, 0, tiled=True)  21.7 us
    all_to_all x1, starting transfers between devices, body(): same = lax.all_to_all(copies, ('yh', 'zh'), 0, 0, tiled=True)  16.2 us
    all_to_all x1, blocking collectives, body(): proj_parts = lax.all_to_all(proj, ('core', 'yl', 'x'), 0, 0, tiled=True)  11.1 us
    all_to_all x1, starting transfers between devices, body(): parts = lax.all_to_all(cross, ('core', 'yl', 'x'), 0, 0, tiled=True)  6.32 us
    all_to_all x1, waiting for transfers between devices, body(): same = lax.all_to_all(copies, ('yh', 'zh'), 0, 0, tiled=True)  5.62 us
    pallas_call x2, Pallas kernels, products(): pl.pallas_call(functools.partial(gram_kernel, quads, other), in_specs=[hb...  5.34 us
    pallas_call x1, Pallas kernels, body(): pl.pallas_call(cross_kernel, grid=(steps,), in_specs=[SMEM_SPEC, pl.Block...  4.54 us
    unnamed x6, local copies, waits for them, and re-layouts  3.98 us
  transfers between devices with their start and end apart: 6, of which 4 were waited for; matrix products, arithmetic and copies ran while one was open for 0% of the time, Pallas kernels for 13%

profile of v5, /device:TPU:1, one launch (start us, length us, event | category | flops | bytes accessed | tf_op | source)
XLA Modules:
  0.0 100.6 jit_solution(7993280930843176706)
XLA Ops:
  0.0 0.7 copy-done.2
  0.7 0.9 vector_copies.1
  1.6 16.2 %all-to-all-start = ((bf16[16,96,128]{2,1,0:T(8,128)(2,1)}), bf16[16,96,128]{2,1,0:T(8,128)(2,1)S(1)}, u32[]{:S(2)}, u32[]{:S(2)}) async-start(bf16[16,96,128]{2,1,0:T(8,128)(2,1)} %vector_copies.1), calls=%async_computation | async-start | bytes 786432 | tf_op jit(solution)/shard_map/all_to_all | solution.py:346
  18.0 2.3 %copy-done = bf16[96,3,8192]{2,0,1:T(8,128)(2,1)S(1)} copy-done((bf16[96,3,8192]{2,0,1:T(8,128)(2,1)S(1)}, bf16[96,3,8192]{2,0,1:T(8,128)(2,1)}, u32[]{:S(2)}) %copy-start) | copy-done | bytes 4718616
  20.3 0.9 copy-done.1
  21.2 4.5 %cross_terms.1 = (bf16[2,288,2048]{2,1,0:T(8,128)(2,1)S(1)}, bf16[2,288,2048]{2,1,0:T(8,128)(2,1)}, bf16[2,16,2048]{2,1,0:T(8,128)(2,1)S(1)}, f32[16,8,304]{2,1,0:T(8,128)}) custom-call(s32[2]{0:T(128)S(1)} %pad_add_fusion.place_ref, bf16[288,8192]{1,0:T(8,128)(2,1)S(1)} %bitcast.15, f32[3,8192]{1,0:T(4,128)S(1)} %copy-done.1), custom_call_target="tpu_custom_call" | custom-call | flops 1207959552 | bytes 9437184 | tf_op jit(solution)/shard_map/cross_terms/pallas_call | solution.py:351
  25.8 2.9 %collective-permute-start = (bf16[2,288,2048]{2,1,0:T(8,128)(2,1)}, bf16[2,288,2048]{2,1,0:T(8,128)(2,1)}, u32[]{:S(2)}, u32[]{:S(2)}) collective-permute-start(bf16[2,288,2048]{2,1,0:T(8,128)(2,1)} %get-tuple-element.21), channel_id=1, source_target_pairs={{0,8},{8,0},{1,9},{9,1},{2,10},{10,2},{3,11},{11,3},{4,12},{12,4},... | collective-permute-start | bytes 7077896 | tf_op jit(solution)/shard_map/ppermute | solution.py:368
  28.6 0.5 pass_core.1.core_ref
  29.1 5.6 %all-to-all-done.vec_ref = bf16[16,96,128]{2,1,0:T(8,128)(2,1)S(1)} async-done(((bf16[16,96,128]{2,1,0:T(8,128)(2,1)}), bf16[16,96,128]{2,1,0:T(8,128)(2,1)S(1)}, u32[]{:S(2)}, u32[]{:S(2)}) %all-to-all-start) | async-done | bytes 393248 | tf_op jit(solution)/shard_map/all_to_all | solution.py:346
  34.8 2.8 %collective-permute-start.1 = (bf16[16,96,128]{2,1,0:T(8,128)(2,1)S(1)}, bf16[16,96,128]{2,1,0:T(8,128)(2,1)S(1)}, u32[]{:S(2)}, u32[]{:S(2)}) collective-permute-start(bf16[16,96,128]{2,1,0:T(8,128)(2,1)S(1)} %all-to-all-done.vec_ref), channel_id=1, source_target_pairs={{0,448},{64,0},{128,64},{192,128},{256,192},{320,256},{384,320},{4... | collective-permute-start | bytes 1179656 | tf_op jit(solution)/shard_map/ppermute | solution.py:378
  37.5 6.3 %all-to-all-start.1 = ((f32[16,8,304]{2,1,0:T(8,128)}), f32[16,8,304]{2,1,0:T(8,128)S(1)}, u32[]{:S(2)}, u32[]{:S(2)}) async-start(f32[16,8,304]{2,1,0:T(8,128)} %get-tuple-element.19.after_ref), calls=%async_computation.1 | async-start | bytes 393216 | tf_op jit(solution)/shard_map/all_to_all | solution.py:379
  43.9 2.7 %vector_products.2.rest_0_ = f32[592,96]{1,0:T(8,128)S(1)} custom-call(bf16[2,288,2048]{2,1,0:T(8,128)(2,1)S(1)} %get-tuple-element.20.keep_hbm, bf16[2,288,2048]{2,1,0:T(8,128)(2,1)} %collective-permute-done.recv_hbm, bf16[2,16,2048]{2,1,0:T(8,128)(2,1)S(1)} %get-tuple-element.22.rows_ref, bf16[16,96,128]{2,1,0:T(8,128)(2,1)S(1)} %all-to-all-done.vec_ref), custom_call_target="tpu_custom_call" | custom-call | flops 1 | bytes 1000000 | tf_op jit(solution)/shard_map/vector_products/pallas_call | solution.py:385
  46.5 2.7 %vector_products.3.gram_ref = f32[592,96]{1,0:T(8,128)S(1)} custom-call(bf16[2,288,2048]{2,1,0:T(8,128)(2,1)S(1)} %get-tuple-element.20.keep_hbm, bf16[2,288,2048]{2,1,0:T(8,128)(2,1)} %collective-permute-done.recv_hbm, bf16[2,16,2048]{2,1,0:T(8,128)(2,1)S(1)} %get-tuple-element.22.rows_ref, bf16[16,96,128]{2,1,0:T(8,128)(2,1)S(1)} %collective-permute-done.1.vec_ref, ...), custom_call_target="tpu_custom_call" | custom-call | flops 1 | bytes 1000000 | tf_op jit(solution)/shard_map/vector_products/pallas_call | solution.py:385
  49.2 1.7 %all-to-all-done.1.parts_ref = f32[16,8,304]{2,1,0:T(8,128)S(1)} async-done(((f32[16,8,304]{2,1,0:T(8,128)}), f32[16,8,304]{2,1,0:T(8,128)S(1)}, u32[]{:S(2)}, u32[]{:S(2)}) %all-to-all-start.1) | async-done | bytes 155680 | tf_op jit(solution)/shard_map/all_to_all | solution.py:379
  50.9 3.3 %rotation_projection.1 = (f32[776,96]{1,0:T(8,128)S(1)}, bf16[16,48,128]{2,1,0:T(8,128)(2,1)S(1)}) custom-call(s32[1]{0:T(128)} %pass_core.1.core_ref, f32[16,8,304]{2,1,0:T(8,128)S(1)} %all-to-all-done.1.parts_ref, f32[592,96]{1,0:T(8,128)S(1)} %vector_products.3.gram_ref), custom_call_target="tpu_custom_call" | custom-call | flops 1000000000 | bytes 1000000 | tf_op jit(solution)/shard_map/rotation_projection/pallas_call | solution.py:400
  54.2 11.1 %all_to_all.20.parts_ref = bf16[16,48,128]{2,1,0:T(8,128)(2,1)S(1)} all-to-all(bf16[16,48,128]{2,1,0:T(8,128)(2,1)S(1)} %get-tuple-element.24), channel_id=1, replica_groups=mesh['zh'=4,'zp'=2,'yh'=4,'core'=2,'yl'=2,'x'=4] {'core','yl','x'}, dimensions={0} | all-to-all | bytes 393216 | tf_op jit(solution)/shard_map/all_to_all | solution.py:412
  65.3 2.4 %product_terms.1 = (bf16[10,96,128]{2,1,0:T(8,128)(2,1)S(1)}, bf16[6,96,128]{2,1,0:T(8,128)(2,1)S(1)}, bf16[288,592]{1,0:T(8,128)(2,1)S(1)}) custom-call(s32[1]{0:T(128)} %bitcast.core_ref, bf16[16,48,128]{2,1,0:T(8,128)(2,1)S(1)} %all_to_all.20.parts_ref, f32[776,96]{1,0:T(8,128)S(1)} %get-tuple-element.25.rot_ref, ...), custom_call_target="tpu_custom_call" | custom-call | flops 1 | bytes 1 | tf_op jit(solution)/shard_map/product_terms/pallas_call | solution.py:414
  67.7 3.2 %collective-permute-start.2 = (bf16[10,96,128]{2,1,0:T(8,128)(2,1)S(1)}, bf16[10,96,128]{2,1,0:T(8,128)(2,1)S(1)}, u32[]{:S(2)}, u32[]{:S(2)}) collective-permute-start(bf16[10,96,128]{2,1,0:T(8,128)(2,1)S(1)} %get-tuple-element.27), channel_id=1, source_target_pairs={{0,64},{64,128},{128,192},{192,256},{256,320},{320,384},{384,448},... | collective-permute-start | bytes 737288 | tf_op jit(solution)/shard_map/ppermute | solution.py:428
  70.9 3.3 %collective-permute-start.3 = (bf16[6,96,128]{2,1,0:T(8,128)(2,1)S(1)}, bf16[6,96,128]{2,1,0:T(8,128)(2,1)S(1)}, u32[]{:S(2)}, u32[]{:S(2)}) collective-permute-start(bf16[6,96,128]{2,1,0:T(8,128)(2,1)S(1)} %get-tuple-element.28), channel_id=1, source_target_pairs={{0,448},{64,0},{128,64},{192,128},{256,192},{320,256},{384,320},{4... | collective-permute-start | bytes 442376 | tf_op jit(solution)/shard_map/ppermute | solution.py:429
  74.3 2.4 %product_terms_same.1 = f32[4,4,96,128]{3,2,1,0:T(8,128)S(1)} custom-call(bf16[288,592]{1,0:T(8,128)(2,1)S(1)} %get-tuple-element.26.weight_ref, bf16[2,288,2048]{2,1,0:T(8,128)(2,1)S(1)} %get-tuple-element.20.keep_hbm, bf16[2,288,2048]{2,1,0:T(8,128)(2,1)} %collective-permute-done.recv_hbm, bf16[2,16,2048]{2,1,0:T(8,128)(2,1)S(1)} %get-tuple-element.22.rows_ref), custom_call_target="tpu_custom_call" | custom-call | flops 1207959552 | bytes 9437184 | tf_op jit(solution)/shard_map/product_terms_same/pallas_call | solution.py:430
  76.7 1.0 %collective-permute-done.3 = bf16[6,96,128]{2,1,0:T(8,128)(2,1)S(1)} collective-permute-done((bf16[6,96,128]{2,1,0:T(8,128)(2,1)S(1)}, bf16[6,96,128]{2,1,0:T(8,128)(2,1)S(1)}, u32[]{:S(2)}, u32[]{:S(2)}) %collective-permute-start.3) | collective-permute-done | bytes 147488 | tf_op jit(solution)/shard_map/ppermute | solution.py:429
  77.7 0.5 collective-permute-done.2
  78.3 21.7 %all_to_all.21 = bf16[16,96,128]{2,1,0:T(8,128)(2,1)S(1)} all-to-all(bf16[16,96,128]{2,1,0:T(8,128)(2,1)S(1)} %fusion), channel_id=1, replica_groups=mesh['zh'=4,'zp'=2,'yh'=4,'core'=2,'yl'=2,'x'=4] {'yh','zh'}, dimensions={0} | all-to-all | bytes 786432 | tf_op jit(solution)/shard_map/all_to_all | solution.py:442
  100.0 0.7 convert_reduce_fusion
  (7 shorter events, 0.2 us)
Async XLA Ops:
  0.0 0.7 copy-start.2
  1.6 33.1 %all-to-all-start = ((bf16[16,96,128]{2,1,0:T(8,128)(2,1)}), bf16[16,96,128]{2,1,0:T(8,128)(2,1)S(1)}, u32[]{:S(2)}, u32[]{:S(2)}) async-start(bf16[16,96,128]{2,1,0:T(8,128)(2,1)} %vector_copies.1), calls=%async_computation | async-start | bytes 786432 | tf_op jit(solution)/shard_map/all_to_all | solution.py:346
  18.0 2.3 %copy-start = (bf16[96,3,8192]{2,0,1:T(8,128)(2,1)S(1)}, bf16[96,3,8192]{2,0,1:T(8,128)(2,1)}, u32[]{:S(2)}) copy-start(bf16[96,3,8192]{2,0,1:T(8,128)(2,1)} %param.3) | copy-start | bytes 14155780
  20.3 0.9 copy-start.1
  25.8 18.1 %collective-permute-start = (bf16[2,288,2048]{2,1,0:T(8,128)(2,1)}, bf16[2,288,2048]{2,1,0:T(8,128)(2,1)}, u32[]{:S(2)}, u32[]{:S(2)}) collective-permute-start(bf16[2,288,2048]{2,1,0:T(8,128)(2,1)} %get-tuple-element.21), channel_id=1, source_target_pairs={{0,8},{8,0},{1,9},{9,1},{2,10},{10,2},{3,11},{11,3},{4,12},{12,4},... | collective-permute-start | bytes 7077896 | tf_op jit(solution)/shard_map/ppermute | solution.py:368
  34.8 11.8 %collective-permute-start.1 = (bf16[16,96,128]{2,1,0:T(8,128)(2,1)S(1)}, bf16[16,96,128]{2,1,0:T(8,128)(2,1)S(1)}, u32[]{:S(2)}, u32[]{:S(2)}) collective-permute-start(bf16[16,96,128]{2,1,0:T(8,128)(2,1)S(1)} %all-to-all-done.vec_ref), channel_id=1, source_target_pairs={{0,448},{64,0},{128,64},{192,128},{256,192},{320,256},{384,320},{4... | collective-permute-start | bytes 1179656 | tf_op jit(solution)/shard_map/ppermute | solution.py:378
  37.5 13.4 %all-to-all-start.1 = ((f32[16,8,304]{2,1,0:T(8,128)}), f32[16,8,304]{2,1,0:T(8,128)S(1)}, u32[]{:S(2)}, u32[]{:S(2)}) async-start(f32[16,8,304]{2,1,0:T(8,128)} %get-tuple-element.19.after_ref), calls=%async_computation.1 | async-start | bytes 393216 | tf_op jit(solution)/shard_map/all_to_all | solution.py:379
  67.7 10.4 %collective-permute-start.2 = (bf16[10,96,128]{2,1,0:T(8,128)(2,1)S(1)}, bf16[10,96,128]{2,1,0:T(8,128)(2,1)S(1)}, u32[]{:S(2)}, u32[]{:S(2)}) collective-permute-start(bf16[10,96,128]{2,1,0:T(8,128)(2,1)S(1)} %get-tuple-element.27), channel_id=1, source_target_pairs={{0,64},{64,128},{128,192},{192,256},{256,320},{320,384},{384,448},... | collective-permute-start | bytes 737288 | tf_op jit(solution)/shard_map/ppermute | solution.py:428
  70.9 6.8 %collective-permute-start.3 = (bf16[6,96,128]{2,1,0:T(8,128)(2,1)S(1)}, bf16[6,96,128]{2,1,0:T(8,128)(2,1)S(1)}, u32[]{:S(2)}, u32[]{:S(2)}) collective-permute-start(bf16[6,96,128]{2,1,0:T(8,128)(2,1)S(1)} %get-tuple-element.28), channel_id=1, source_target_pairs={{0,448},{64,0},{128,64},{192,128},{256,192},{320,256},{384,320},{4... | collective-permute-start | bytes 442376 | tf_op jit(solution)/shard_map/ppermute | solution.py:429

commit v6 on v5

--- a/solution.py
+++ b/solution.py
@@ -74,7 +74,7 @@
         row, col = iota((8, EXTRA), 0), iota((8, EXTRA), 1)
         pick = ((row < 3) & (col < 9) & ((col == row) | (col == row + 3) | (col == row + 6))) | ((row == 3) & (col == 9))
         cross = lax.dot_general(pick.astype(F32), total, NT, precision=HIGHEST, preferred_element_type=F32)
-        cross_ref[...] = jnp.broadcast_to(cross[None], cross_ref.shape)
+        cross_ref[...] = jnp.broadcast_to(cross[None, :4], cross_ref.shape)
 
 
 def polar_factor(amat):
@@ -356,9 +356,9 @@
             pl.BlockSpec((rows, wide), lambda step: (0, step)),
             pl.BlockSpec((3, wide), lambda step: (0, step)),
         ],
-        out_specs=[both(rows), both(rows), both(EXTRA), whole(peers, 8, rows + EXTRA)],
+        out_specs=[both(rows), both(rows), both(EXTRA), whole(peers, 4, rows + EXTRA)],
         out_shape=[
-            sorted_shape(rows), sorted_shape(rows), sorted_shape(EXTRA), jax.ShapeDtypeStruct((peers, 8, rows + EXTRA), F32),
+            sorted_shape(rows), sorted_shape(rows), sorted_shape(EXTRA), jax.ShapeDtypeStruct((peers, 4, rows + EXTRA), F32),
         ],
         scratch_shapes=[pltpu.VMEM((rows + EXTRA, EXTRA), F32)],
         compiler_params=params(),

time: 101 us -> 101 us (level)
  blocking collectives: 32.8 us -> 33.9 us
    all_to_all x1, blocking collectives: 11.1 us -> 12.2 us  [body(): proj_parts = lax.all_to_all(proj, ('core', 'yl', 'x'), 0, 0, tiled=True)]
    all_to_all x1, waiting for transfers between devices: 1.67 us -> 0.63 us  [body(): parts = lax.all_to_all(cross, ('core', 'yl', 'x'), 0, 0, tiled=True)]
where the time goes in v6:
time: 101 us; the launch traced here: 100 us
  starting transfers between devices  34.7 us (34%)
  blocking collectives  33.9 us (34%)
  Pallas kernels  19.1 us (19%)
  waiting for transfers between devices  7.8 us (8%)
  local copies, waits for them, and re-layouts  3.98 us (4%)
    all_to_all x1, blocking collectives, body(): terms = lax.all_to_all(term, ('yh', 'zh'), 0, 0, tiled=True)  21.7 us
    all_to_all x1, starting transfers between devices, body(): same = lax.all_to_all(copies, ('yh', 'zh'), 0, 0, tiled=True)  16.2 us
    all_to_all x1, blocking collectives, body(): proj_parts = lax.all_to_all(proj, ('core', 'yl', 'x'), 0, 0, tiled=True)  12.2 us
    all_to_all x1, starting transfers between devices, body(): parts = lax.all_to_all(cross, ('core', 'yl', 'x'), 0, 0, tiled=True)  6.32 us
    all_to_all x1, waiting for transfers between devices, body(): same = lax.all_to_all(copies, ('yh', 'zh'), 0, 0, tiled=True)  5.66 us
    pallas_call x2, Pallas kernels, products(): pl.pallas_call(functools.partial(gram_kernel, quads, other), in_specs=[hb...  5.34 us
    pallas_call x1, Pallas kernels, body(): pl.pallas_call(cross_kernel, grid=(steps,), in_specs=[SMEM_SPEC, pl.Block...  4.51 us
    unnamed x6, local copies, waits for them, and re-layouts  3.98 us
  transfers between devices with their start and end apart: 6, of which 4 were waited for; matrix products, arithmetic and copies ran while one was open for 0% of the time, Pallas kernels for 13%

profile of v6, /device:TPU:1, one launch (start us, length us, event | category | flops | bytes accessed | tf_op | source)
XLA Modules:
  0.0 100.3 jit_solution(9389581980795038550)
XLA Ops:
  0.0 0.7 copy-done.2
  0.7 0.9 vector_copies.1
  1.6 16.2 %all-to-all-start = ((bf16[16,96,128]{2,1,0:T(8,128)(2,1)}), bf16[16,96,128]{2,1,0:T(8,128)(2,1)S(1)}, u32[]{:S(2)}, u32[]{:S(2)}) async-start(bf16[16,96,128]{2,1,0:T(8,128)(2,1)} %vector_copies.1), calls=%async_computation | async-start | bytes 786432 | tf_op jit(solution)/shard_map/all_to_all | solution.py:346
  18.0 2.3 %copy-done = bf16[96,3,8192]{2,0,1:T(8,128)(2,1)S(1)} copy-done((bf16[96,3,8192]{2,0,1:T(8,128)(2,1)S(1)}, bf16[96,3,8192]{2,0,1:T(8,128)(2,1)}, u32[]{:S(2)}) %copy-start) | copy-done | bytes 4718616
  20.3 0.9 copy-done.1
  21.2 4.5 %cross_terms.1 = (bf16[2,288,2048]{2,1,0:T(8,128)(2,1)S(1)}, bf16[2,288,2048]{2,1,0:T(8,128)(2,1)}, bf16[2,16,2048]{2,1,0:T(8,128)(2,1)S(1)}, f32[16,4,304]{2,1,0:T(4,128)}) custom-call(s32[2]{0:T(128)S(1)} %pad_add_fusion.place_ref, bf16[288,8192]{1,0:T(8,128)(2,1)S(1)} %bitcast.15, f32[3,8192]{1,0:T(4,128)S(1)} %copy-done.1), custom_call_target="tpu_custom_call" | custom-call | flops 1207959552 | bytes 9437184 | tf_op jit(solution)/shard_map/cross_terms/pallas_call | solution.py:351
  25.7 2.9 %collective-permute-start = (bf16[2,288,2048]{2,1,0:T(8,128)(2,1)}, bf16[2,288,2048]{2,1,0:T(8,128)(2,1)}, u32[]{:S(2)}, u32[]{:S(2)}) collective-permute-start(bf16[2,288,2048]{2,1,0:T(8,128)(2,1)} %get-tuple-element.21), channel_id=1, source_target_pairs={{0,8},{8,0},{1,9},{9,1},{2,10},{10,2},{3,11},{11,3},{4,12},{12,4},... | collective-permute-start | bytes 7077896 | tf_op jit(solution)/shard_map/ppermute | solution.py:368
  28.6 0.5 pass_core.1.core_ref
  29.1 5.7 %all-to-all-done.vec_ref = bf16[16,96,128]{2,1,0:T(8,128)(2,1)S(1)} async-done(((bf16[16,96,128]{2,1,0:T(8,128)(2,1)}), bf16[16,96,128]{2,1,0:T(8,128)(2,1)S(1)}, u32[]{:S(2)}, u32[]{:S(2)}) %all-to-all-start) | async-done | bytes 393248 | tf_op jit(solution)/shard_map/all_to_all | solution.py:346
  34.8 2.8 %collective-permute-start.1 = (bf16[16,96,128]{2,1,0:T(8,128)(2,1)S(1)}, bf16[16,96,128]{2,1,0:T(8,128)(2,1)S(1)}, u32[]{:S(2)}, u32[]{:S(2)}) collective-permute-start(bf16[16,96,128]{2,1,0:T(8,128)(2,1)S(1)} %all-to-all-done.vec_ref), channel_id=1, source_target_pairs={{0,448},{64,0},{128,64},{192,128},{256,192},{320,256},{384,320},{4... | collective-permute-start | bytes 1179656 | tf_op jit(solution)/shard_map/ppermute | solution.py:378
  37.5 6.3 %all-to-all-start.1 = ((f32[16,4,304]{2,1,0:T(4,128)}), f32[16,4,304]{2,1,0:T(4,128)S(1)}, u32[]{:S(2)}, u32[]{:S(2)}) async-start(f32[16,4,304]{2,1,0:T(4,128)} %get-tuple-element.19.after_ref), calls=%async_computation.1 | async-start | bytes 196608 | tf_op jit(solution)/shard_map/all_to_all | solution.py:379
  43.9 2.7 %vector_products.2.rest_0_ = f32[592,96]{1,0:T(8,128)S(1)} custom-call(bf16[2,288,2048]{2,1,0:T(8,128)(2,1)S(1)} %get-tuple-element.20.keep_hbm, bf16[2,288,2048]{2,1,0:T(8,128)(2,1)} %collective-permute-done.recv_hbm, bf16[2,16,2048]{2,1,0:T(8,128)(2,1)S(1)} %get-tuple-element.22.rows_ref, bf16[16,96,128]{2,1,0:T(8,128)(2,1)S(1)} %all-to-all-done.vec_ref), custom_call_target="tpu_custom_call" | custom-call | flops 1 | bytes 1000000 | tf_op jit(solution)/shard_map/vector_products/pallas_call | solution.py:385
  46.5 2.7 %vector_products.3.gram_ref = f32[592,96]{1,0:T(8,128)S(1)} custom-call(bf16[2,288,2048]{2,1,0:T(8,128)(2,1)S(1)} %get-tuple-element.20.keep_hbm, bf16[2,288,2048]{2,1,0:T(8,128)(2,1)} %collective-permute-done.recv_hbm, bf16[2,16,2048]{2,1,0:T(8,128)(2,1)S(1)} %get-tuple-element.22.rows_ref, bf16[16,96,128]{2,1,0:T(8,128)(2,1)S(1)} %collective-permute-done.1.vec_ref, ...), custom_call_target="tpu_custom_call" | custom-call | flops 1 | bytes 1000000 | tf_op jit(solution)/shard_map/vector_products/pallas_call | solution.py:385
  49.2 0.6 all-to-all-done.1.parts_ref
  49.9 3.0 %rotation_projection.1 = (f32[776,96]{1,0:T(8,128)S(1)}, bf16[16,48,128]{2,1,0:T(8,128)(2,1)S(1)}) custom-call(s32[1]{0:T(128)} %pass_core.1.core_ref, f32[16,4,304]{2,1,0:T(4,128)S(1)} %all-to-all-done.1.parts_ref, f32[592,96]{1,0:T(8,128)S(1)} %vector_products.3.gram_ref), custom_call_target="tpu_custom_call" | custom-call | flops 1000000000 | bytes 1000000 | tf_op jit(solution)/shard_map/rotation_projection/pallas_call | solution.py:400
  52.9 12.2 %all_to_all.20.parts_ref = bf16[16,48,128]{2,1,0:T(8,128)(2,1)S(1)} all-to-all(bf16[16,48,128]{2,1,0:T(8,128)(2,1)S(1)} %get-tuple-element.24), channel_id=1, replica_groups=mesh['zh'=4,'zp'=2,'yh'=4,'core'=2,'yl'=2,'x'=4] {'core','yl','x'}, dimensions={0} | all-to-all | bytes 393216 | tf_op jit(solution)/shard_map/all_to_all | solution.py:412
  65.0 2.4 %product_terms.1 = (bf16[10,96,128]{2,1,0:T(8,128)(2,1)S(1)}, bf16[6,96,128]{2,1,0:T(8,128)(2,1)S(1)}, bf16[288,592]{1,0:T(8,128)(2,1)S(1)}) custom-call(s32[1]{0:T(128)} %bitcast.core_ref, bf16[16,48,128]{2,1,0:T(8,128)(2,1)S(1)} %all_to_all.20.parts_ref, f32[776,96]{1,0:T(8,128)S(1)} %get-tuple-element.25.rot_ref, ...), custom_call_target="tpu_custom_call" | custom-call | flops 1 | bytes 1 | tf_op jit(solution)/shard_map/product_terms/pallas_call | solution.py:414
  67.4 3.2 %collective-permute-start.2 = (bf16[10,96,128]{2,1,0:T(8,128)(2,1)S(1)}, bf16[10,96,128]{2,1,0:T(8,128)(2,1)S(1)}, u32[]{:S(2)}, u32[]{:S(2)}) collective-permute-start(bf16[10,96,128]{2,1,0:T(8,128)(2,1)S(1)} %get-tuple-element.27), channel_id=1, source_target_pairs={{0,64},{64,128},{128,192},{192,256},{256,320},{320,384},{384,448},... | collective-permute-start | bytes 737288 | tf_op jit(solution)/shard_map/ppermute | solution.py:428
  70.6 3.3 %collective-permute-start.3 = (bf16[6,96,128]{2,1,0:T(8,128)(2,1)S(1)}, bf16[6,96,128]{2,1,0:T(8,128)(2,1)S(1)}, u32[]{:S(2)}, u32[]{:S(2)}) collective-permute-start(bf16[6,96,128]{2,1,0:T(8,128)(2,1)S(1)} %get-tuple-element.28), channel_id=1, source_target_pairs={{0,448},{64,0},{128,64},{192,128},{256,192},{320,256},{384,320},{4... | collective-permute-start | bytes 442376 | tf_op jit(solution)/shard_map/ppermute | solution.py:429
  73.9 2.4 %product_terms_same.1 = f32[4,4,96,128]{3,2,1,0:T(8,128)S(1)} custom-call(bf16[288,592]{1,0:T(8,128)(2,1)S(1)} %get-tuple-element.26.weight_ref, bf16[2,288,2048]{2,1,0:T(8,128)(2,1)S(1)} %get-tuple-element.20.keep_hbm, bf16[2,288,2048]{2,1,0:T(8,128)(2,1)} %collective-permute-done.recv_hbm, bf16[2,16,2048]{2,1,0:T(8,128)(2,1)S(1)} %get-tuple-element.22.rows_ref), custom_call_target="tpu_custom_call" | custom-call | flops 1207959552 | bytes 9437184 | tf_op jit(solution)/shard_map/product_terms_same/pallas_call | solution.py:430
  76.4 1.0 %collective-permute-done.3 = bf16[6,96,128]{2,1,0:T(8,128)(2,1)S(1)} collective-permute-done((bf16[6,96,128]{2,1,0:T(8,128)(2,1)S(1)}, bf16[6,96,128]{2,1,0:T(8,128)(2,1)S(1)}, u32[]{:S(2)}, u32[]{:S(2)}) %collective-permute-start.3) | collective-permute-done | bytes 147488 | tf_op jit(solution)/shard_map/ppermute | solution.py:429
  77.4 0.5 collective-permute-done.2
  78.0 21.7 %all_to_all.21 = bf16[16,96,128]{2,1,0:T(8,128)(2,1)S(1)} all-to-all(bf16[16,96,128]{2,1,0:T(8,128)(2,1)S(1)} %fusion), channel_id=1, replica_groups=mesh['zh'=4,'zp'=2,'yh'=4,'core'=2,'yl'=2,'x'=4] {'yh','zh'}, dimensions={0} | all-to-all | bytes 786432 | tf_op jit(solution)/shard_map/all_to_all | solution.py:442
  99.6 0.7 convert_reduce_fusion
  (7 shorter events, 0.2 us)
Async XLA Ops:
  0.0 0.7 copy-start.2
  1.6 33.1 %all-to-all-start = ((bf16[16,96,128]{2,1,0:T(8,128)(2,1)}), bf16[16,96,128]{2,1,0:T(8,128)(2,1)S(1)}, u32[]{:S(2)}, u32[]{:S(2)}) async-start(bf16[16,96,128]{2,1,0:T(8,128)(2,1)} %vector_copies.1), calls=%async_computation | async-start | bytes 786432 | tf_op jit(solution)/shard_map/all_to_all | solution.py:346
  18.0 2.3 %copy-start = (bf16[96,3,8192]{2,0,1:T(8,128)(2,1)S(1)}, bf16[96,3,8192]{2,0,1:T(8,128)(2,1)}, u32[]{:S(2)}) copy-start(bf16[96,3,8192]{2,0,1:T(8,128)(2,1)} %param.3) | copy-start | bytes 14155780
  20.3 0.9 copy-start.1
  25.7 18.1 %collective-permute-start = (bf16[2,288,2048]{2,1,0:T(8,128)(2,1)}, bf16[2,288,2048]{2,1,0:T(8,128)(2,1)}, u32[]{:S(2)}, u32[]{:S(2)}) collective-permute-start(bf16[2,288,2048]{2,1,0:T(8,128)(2,1)} %get-tuple-element.21), channel_id=1, source_target_pairs={{0,8},{8,0},{1,9},{9,1},{2,10},{10,2},{3,11},{11,3},{4,12},{12,4},... | collective-permute-start | bytes 7077896 | tf_op jit(solution)/shard_map/ppermute | solution.py:368
  34.8 11.8 %collective-permute-start.1 = (bf16[16,96,128]{2,1,0:T(8,128)(2,1)S(1)}, bf16[16,96,128]{2,1,0:T(8,128)(2,1)S(1)}, u32[]{:S(2)}, u32[]{:S(2)}) collective-permute-start(bf16[16,96,128]{2,1,0:T(8,128)(2,1)S(1)} %all-to-all-done.vec_ref), channel_id=1, source_target_pairs={{0,448},{64,0},{128,64},{192,128},{256,192},{320,256},{384,320},{4... | collective-permute-start | bytes 1179656 | tf_op jit(solution)/shard_map/ppermute | solution.py:378
  37.5 12.3 %all-to-all-start.1 = ((f32[16,4,304]{2,1,0:T(4,128)}), f32[16,4,304]{2,1,0:T(4,128)S(1)}, u32[]{:S(2)}, u32[]{:S(2)}) async-start(f32[16,4,304]{2,1,0:T(4,128)} %get-tuple-element.19.after_ref), calls=%async_computation.1 | async-start | bytes 196608 | tf_op jit(solution)/shard_map/all_to_all | solution.py:379
  67.4 10.4 %collective-permute-start.2 = (bf16[10,96,128]{2,1,0:T(8,128)(2,1)S(1)}, bf16[10,96,128]{2,1,0:T(8,128)(2,1)S(1)}, u32[]{:S(2)}, u32[]{:S(2)}) collective-permute-start(bf16[10,96,128]{2,1,0:T(8,128)(2,1)S(1)} %get-tuple-element.27), channel_id=1, source_target_pairs={{0,64},{64,128},{128,192},{192,256},{256,320},{320,384},{384,448},... | collective-permute-start | bytes 737288 | tf_op jit(solution)/shard_map/ppermute | solution.py:428
  70.6 6.8 %collective-permute-start.3 = (bf16[6,96,128]{2,1,0:T(8,128)(2,1)S(1)}, bf16[6,96,128]{2,1,0:T(8,128)(2,1)S(1)}, u32[]{:S(2)}, u32[]{:S(2)}) collective-permute-start(bf16[6,96,128]{2,1,0:T(8,128)(2,1)S(1)} %get-tuple-element.28), channel_id=1, source_target_pairs={{0,448},{64,0},{128,64},{192,128},{256,192},{320,256},{384,320},{4... | collective-permute-start | bytes 442376 | tf_op jit(solution)/shard_map/ppermute | solution.py:429
